TPU v7x, 256 devices: a whole 4x4x8 slice. The times are simulated.
256 devices in a mesh: dp: 32 (over y_lo, z, core), tensor: 8 (over y_hi, x).
Axes of the slice: x: 4, y: 4 (y_hi: 2, y_lo: 2; y = y_hi * 2 + y_lo), z: 8, core: 2. Of those that a mesh axis runs over, the one named last changes fastest.
Arguments:
- context: bfloat16 [49152, 5120], P(('dp', 'tensor')), may hold values from -6 to 6
- residual: bfloat16 [49152, 10240], P(('dp', 'tensor')), may hold values from -128 to 128
- out_weight: bfloat16 [5120, 10240], P('dp', 'tensor'), may hold values from -0.078125 to 0.078125
- norm_gain: float32 [10240], P('tensor'), may hold values from 0.5 to 1.5
- norm_bias: float32 [10240], P('tensor'), may hold values from -3 to 3
- head_weight: bfloat16 [10240, 128], P('tensor'), may hold values from -0.207524471 to 0.207524471
- targets: int32 [49152], P(('dp', 'tensor')), may hold values from 0 to 127
- packing: int32 [2, 49152], P(None, ('dp', 'tensor')), may hold values from -1 to 95, as said below
- lengths: int32 [1024], P(('dp', 'tensor')), may hold values from 0 to 192, as said below
Outputs:
- residue_scores: float32 [49152], P(('dp', 'tensor'))
- packed_scores: float32 [24576], P(('dp', 'tensor'))
- protein_scores: float32 [1024], P(('dp', 'tensor'))
Inputs may be any that keep to these rules, and one draw needn't show every extreme that they name: Row r of owner block d = r // 192 (blocks in mesh order, dp slowest) is live where packing[0, r] >= 0, and then goes to data group packing[0, r] in lane d % 8 at packed row packing[1, r]; dead rows hold -1 in both. Live rows of a block come first, their count is 0 to 192 with both ends reached. Every packed row of every group and lane receives exactly one live row. From one owner block to one group at most 6 rows, reached in every draw. The 4 lengths of a block sum to the block's count of live rows; a length may be 0.
All inputs are finite; a program needn't handle non-finite values.
Results may differ from a plain program's by a relative error of at most 0.0003.
Values may be sent and summed in bfloat16 or wider, within the bound.
A program may use at most 128 MiB of HBM per device.

v0:
```python
import jax
import jax.numpy as jnp
from jax import lax
from jax.sharding import PartitionSpec as P

GROUP_DEV = 96


epsilon = 1e-05


def send_layout(dest_group, group_count, slot_width):
    own_rows = dest_group.shape[0]
    member_grid = (dest_group[:, None] == jnp.arange(group_count, dtype=jnp.int32)[None, :]).astype(
        jnp.int32
    )
    earlier = jnp.cumsum(member_grid, axis=0) - member_grid
    rank_in = jnp.sum(earlier * member_grid, axis=1)
    places = jnp.where(dest_group >= 0, dest_group * slot_width + rank_in, group_count * slot_width)
    source_index = (
        jnp.full((group_count * slot_width + 1,), own_rows, jnp.int32)
        .at[places]
        .set(jnp.arange(own_rows, dtype=jnp.int32))
    )
    return (source_index[: group_count * slot_width], places)


def receive_layout(offsets, group_rows):
    slot_total = offsets.shape[0]
    targets_at = jnp.where(offsets >= 0, offsets, group_rows)
    return (
        jnp.zeros((group_rows + 1,), jnp.int32)
        .at[targets_at]
        .set(jnp.arange(slot_total, dtype=jnp.int32))[:group_rows]
    )


def score_rows(
    context_rows, residual_rows, target_rows, out_weight, norm_gain, norm_bias, head_weight
):
    width_full = residual_rows.shape[1]
    all_context = lax.all_gather(context_rows, "tensor", axis=0, tiled=True)
    column_rows = lax.all_to_all(residual_rows, "tensor", split_axis=1, concat_axis=0, tiled=True)
    hidden = column_rows.astype(jnp.float32) + jnp.dot(
        all_context,
        lax.all_gather(out_weight, "dp", axis=0, tiled=True),
        preferred_element_type=jnp.float32,
    )
    head_float = head_weight.astype(jnp.float32)
    row_sum = jnp.sum(hidden, axis=1)
    row_square = jnp.sum(hidden * hidden, axis=1)
    total_sum, total_square = lax.psum((row_sum, row_square), "tensor")
    center = total_sum / width_full
    spread = total_square / width_full - center * center
    inverse_std = lax.rsqrt(spread + epsilon)
    normed = (hidden - center[:, None]) * inverse_std[:, None] * norm_gain + norm_bias
    logits = lax.psum_scatter(
        jnp.dot(normed, head_float, precision=lax.Precision.HIGHEST),
        "tensor",
        scatter_dimension=0,
        tiled=True,
    )
    largest = jnp.max(logits, axis=1, keepdims=True)
    log_total = largest[:, 0] + jnp.log(jnp.sum(jnp.exp(logits - largest), axis=1))
    token_ids = jnp.arange(logits.shape[1], dtype=jnp.int32)
    picked = jnp.sum(jnp.where(token_ids[None, :] == target_rows[:, None], logits, 0.0), axis=1)
    return picked - log_total


def shards(
    context, residual, out_weight, norm_gain, norm_bias, head_weight, targets, packing, lengths
):
    group_count = lax.axis_size("dp")
    own_rows = context.shape[0]
    ctx_width = context.shape[1]
    model_width = residual.shape[1]
    slot_width = own_rows // group_count
    dest_group = packing[0]
    dest_offset = packing[1]
    live_rows = dest_group >= 0
    source_index, places = send_layout(dest_group, group_count, slot_width)
    filled = source_index < own_rows
    safe_index = jnp.minimum(source_index, own_rows - 1)
    safe_place = jnp.minimum(places, group_count * slot_width - 1)
    send_context = context[safe_index].reshape(group_count, slot_width, ctx_width)
    send_residual = residual[safe_index].reshape(group_count, slot_width, model_width)
    send_labels = jnp.stack(
        [targets[safe_index], jnp.where(filled, dest_offset[safe_index], -1)], axis=1
    ).reshape(group_count, slot_width, 2)
    got_context, got_residual = (
        lax.all_to_all(send_context, "dp", split_axis=0, concat_axis=0, tiled=True),
        lax.all_to_all(send_residual, "dp", split_axis=0, concat_axis=0, tiled=True),
    )
    got_labels = lax.all_to_all(send_labels, "dp", split_axis=0, concat_axis=0, tiled=True).reshape(
        group_count * slot_width, 2
    )
    got_offsets = got_labels[:, 1]
    pick_rows = receive_layout(got_offsets, GROUP_DEV)
    packed_scores = score_rows(
        got_context.reshape(-1, ctx_width)[pick_rows],
        got_residual.reshape(-1, model_width)[pick_rows],
        got_labels[:, 0][pick_rows],
        out_weight,
        norm_gain,
        norm_bias,
        head_weight,
    )
    safe_offsets = jnp.clip(got_offsets, 0, GROUP_DEV - 1)
    returning = jnp.where(got_offsets >= 0, packed_scores[safe_offsets], 0.0).reshape(
        group_count, slot_width
    )
    came_back = lax.all_to_all(returning, "dp", split_axis=0, concat_axis=0, tiled=True).reshape(
        group_count * slot_width
    )
    residue_scores = jnp.where(live_rows, came_back[safe_place], 0.0)
    end_rows = jnp.cumsum(lengths)
    start_rows = end_rows - lengths
    positions = jnp.arange(own_rows, dtype=jnp.int32)
    member = (
        (positions[None, :] >= start_rows[:, None]) & (positions[None, :] < end_rows[:, None])
    ).astype(jnp.float32)
    protein_sums = jnp.dot(member, residue_scores, precision=lax.Precision.HIGHEST)
    protein_scores = protein_sums / jnp.maximum(lengths, 1).astype(jnp.float32)
    return (residue_scores, packed_scores, protein_scores)


def solution(mesh):
    placed = (
        P(("dp", "tensor"), None),
        P(("dp", "tensor"), None),
        P("dp", "tensor"),
        P("tensor"),
        P("tensor"),
        P("tensor", None),
        P(("dp", "tensor")),
        P(None, ("dp", "tensor")),
        P(("dp", "tensor")),
    )
    return jax.shard_map(
        shards,
        mesh=mesh,
        in_specs=placed,
        out_specs=(P(("dp", "tensor")), P(("dp", "tensor")), P(("dp", "tensor"))),
        check_vma=False,
    )
```

profile of v0, /device:TPU:1, one launch (start us, length us, event | category | flops | bytes accessed | tf_op | source)
XLA Modules:
  0.0 498.6 jit_solution(8195037056148414570)
XLA Ops:
  10.9 1.6 gather_fusion.1
  12.7 2.0 gather_fusion
  15.4 11.1 %all-to-all-start = ((s32[32,6,2]{1,2,0:T(2,128)}), s32[32,6,2]{1,2,0:T(2,128)S(1)}, u32[]{:S(2)}, u32[]{:S(2)}) async-start(s32[32,6,2]{1,2,0:T(2,128)} %copy.26), calls=%async_computation | async-start | bytes 65536 | tf_op jit(solution)/shard_map/all_to_all | solution.py:94
  26.5 3.0 gather_fusion.5
  29.5 4.1 reshape.191
  34.5 7.5 %all-to-all-start.3 = ((bf16[32,6,5120]{2,1,0:T(8,128)(2,1)}), bf16[32,6,5120]{2,1,0:T(8,128)(2,1)}, u32[]{:S(2)}, u32[]{:S(2)}) async-start(bf16[32,6,5120]{2,1,0:T(8,128)(2,1)} %reshape.191), calls=%async_computation.3 | async-start | bytes 5242880 | tf_op jit(solution)/shard_map/all_to_all | solution.py:91
  43.4 59.5 %all-to-all-done.3 = bf16[32,6,5120]{2,1,0:T(8,128)(2,1)} async-done(((bf16[32,6,5120]{2,1,0:T(8,128)(2,1)}), bf16[32,6,5120]{2,1,0:T(8,128)(2,1)}, u32[]{:S(2)}, u32[]{:S(2)}) %all-to-all-start.3) | async-done | bytes 1966112 | tf_op jit(solution)/shard_map/all_to_all | solution.py:91
  102.9 2.8 reshape.192
  105.6 2.1 gather_fusion.6
  108.7 11.1 %gather_fusion.3 = bf16[192,10240]{1,0:T(8,128)(2,1)} fusion(bf16[192,10240]{1,0:T(8,128)(2,1)} %param.10, s32[1024]{0:T(1024)S(1)} %pad_clamp_fusion.3), kind=kCustom, calls=%fused_computation.3 | custom fusion | bytes 7865088 | tf_op jit(solution)/shard_map/gather | solution.py:86
  119.8 7.4 %reshape.189 = bf16[32,6,10240]{2,1,0:T(8,128)(2,1)} reshape(bf16[192,10240]{1,0:T(8,128)(2,1)} %gather_fusion.3) | data formatting | bytes 7864320 | tf_op jit(solution)/shard_map/reshape | solution.py:86
  127.2 122.6 %all_to_all.34 = bf16[32,6,10240]{2,1,0:T(8,128)(2,1)} all-to-all(bf16[32,6,10240]{2,1,0:T(8,128)(2,1)} %reshape.189), channel_id=1, replica_groups=mesh['dp'=32,'tensor'=8] {'dp'}, dimensions={0} | all-to-all | bytes 7864320 | tf_op jit(solution)/shard_map/all_to_all | solution.py:92
  249.8 7.3 %reshape.190 = bf16[192,10240]{1,0:T(8,128)(2,1)} reshape(bf16[32,6,10240]{2,1,0:T(8,128)(2,1)} %all_to_all.34) | data formatting | bytes 7864320 | tf_op jit(solution)/shard_map/reshape | solution.py:101
  257.1 6.1 %gather_fusion.4 = bf16[96,10240]{1,0:T(8,128)(2,1)S(1)} fusion(bf16[192,10240]{1,0:T(8,128)(2,1)} %reshape.190, s32[1024]{0:T(1024)S(1)} %pad_clamp_fusion.2), kind=kCustom, calls=%fused_computation.4 | custom fusion | bytes 3932544 | tf_op jit(solution)/shard_map/gather | solution.py:101
  263.4 35.8 %all_to_all.35 = bf16[96,8,1280]{2,0,1:T(8,128)(2,1)S(1)} all-to-all(bf16[96,8,1280]{2,0,1:T(8,128)(2,1)S(1)} %bitcast.53), channel_id=1, replica_groups=mesh['dp'=32,'tensor'=8] {'tensor'}, dimensions={1} | all-to-all | bytes 3932160 | tf_op jit(solution)/shard_map/all_to_all | solution.py:43
  299.2 2.2 convert_element_type.24
  301.4 49.1 %all-gather.4.cloned.1.call-done = bf16[5120,1280]{1,0:T(8,128)(2,1)} async-done(((bf16[160,1280]{1,0:T(8,128)(2,1)}), bf16[5120,1280]{1,0:T(8,128)(2,1)}) %all-gather.4.cloned.1.call-update) | async-done | bytes 13107216 | tf_op jit(solution)/shard_map/all_gather | solution.py:46
  350.6 18.0 %fusion.20 = (f32[768]{0:T(1024)S(1)}, f32[768]{0:T(1024)S(1)}, f32[768,1280]{1,0:T(8,128)}) fusion(f32[768,1280]{1,0:T(8,128)} %bitcast.54, bf16[768,5120]{1,0:T(8,128)(2,1)} %all-gather.6.cloned.1.call-done, bf16[5120,1280]{1,0:T(8,128)(2,1)} %all-gather.4.cloned.1.call-done), kind=kOutput, calls=%fused_computation.69 | convolution fusion | flops 10070259712 | bytes 28841984 | tf_op jit(solution)/shard_map/dot_general | solution.py:44
  368.5 20.3 %all-reduce.1 = (f32[768]{0:T(1024)S(1)}, f32[768]{0:T(1024)S(1)}) all-reduce(f32[768]{0:T(1024)S(1)} %get-tuple-element.4, f32[768]{0:T(1024)S(1)} %get-tuple-element.3), channel_id=1, replica_groups=mesh['dp'=32,'tensor'=8] {'tensor'}, use_global_device_ids=true, to_apply=%region_8.9 | all-reduce | flops 1536 | bytes 12288 | tf_op jit(solution)/shard_map/psum | solution.py:52
  388.9 5.4 %fusion = f32[768,128]{1,0:T(8,128)} fusion(bf16[1280,128]{1,0:T(8,128)(2,1)S(1)} %copy-done.4, f32[768,1280]{1,0:T(8,128)} %get-tuple-element.18, f32[1280]{0:T(1024)S(1)} %copy-done.5, f32[1280]{0:T(1024)S(1)} %copy-done.6, f32[768]{0:T(1024)S(1)} %get-tuple-element.12, f32[768]{0:T(1024)S(1)} %get-tuple-element.11), kind=kOutput, calls=%fused_computation.12 | convolution fusion | flops 1513881600 | bytes 4669440 | tf_op jit(solution)/shard_map/dot_general | solution.py:58
  395.9 70.4 %reduce-scatter.2.cloned.1.call-done = f32[96,128]{1,0:T(8,128)} async-done(((f32[768,128]{1,0:T(8,128)}), f32[96,128]{1,0:T(8,128)}) %reduce-scatter.2.cloned.1.call-update) | async-done | bytes 49168 | tf_op jit(solution)/shard_map/reduce_scatter | solution.py:57
  470.5 10.0 %all-to-all-start.4 = ((f32[32,1,6]{2,1,0:T(1,128)}), f32[32,1,6]{2,1,0:T(1,128)S(1)}, u32[]{:S(2)}, u32[]{:S(2)}) async-start(f32[32,1,6]{2,1,0:T(1,128)} %bitcast.12), calls=%async_computation.5 | async-start | bytes 32768 | tf_op jit(solution)/shard_map/all_to_all | solution.py:112
  480.6 7.8 %all-to-all-done.4 = f32[32,1,6]{2,1,0:T(1,128)S(1)} async-done(((f32[32,1,6]{2,1,0:T(1,128)}), f32[32,1,6]{2,1,0:T(1,128)S(1)}, u32[]{:S(2)}, u32[]{:S(2)}) %all-to-all-start.4) | async-done | bytes 800 | tf_op jit(solution)/shard_map/all_to_all | solution.py:112
  489.7 1.6 gather_fusion.8
  (71 shorter events, 15.7 us)
Async XLA Ops:
  7.2 19.4 %copy-start = (bf16[192,5120]{1,0:T(8,128)(2,1)S(1)}, bf16[192,5120]{1,0:T(8,128)(2,1)}, u32[]{:S(2)}) copy-start(bf16[192,5120]{1,0:T(8,128)(2,1)} %param.9) | copy-start | bytes 5898244
  15.4 19.1 %all-to-all-start = ((s32[32,6,2]{1,2,0:T(2,128)}), s32[32,6,2]{1,2,0:T(2,128)S(1)}, u32[]{:S(2)}, u32[]{:S(2)}) async-start(s32[32,6,2]{1,2,0:T(2,128)} %copy.26), calls=%async_computation | async-start | bytes 65536 | tf_op jit(solution)/shard_map/all_to_all | solution.py:94
  34.5 68.4 %all-to-all-start.3 = ((bf16[32,6,5120]{2,1,0:T(8,128)(2,1)}), bf16[32,6,5120]{2,1,0:T(8,128)(2,1)}, u32[]{:S(2)}, u32[]{:S(2)}) async-start(bf16[32,6,5120]{2,1,0:T(8,128)(2,1)} %reshape.191), calls=%async_computation.3 | async-start | bytes 5242880 | tf_op jit(solution)/shard_map/all_to_all | solution.py:91
  42.0 259.4 %all-gather.6.cloned.1.call-start = ((), (), s32[]{:S(2)}) async-start(), calls=%async_computation.8 | async-start | bytes 8847360 | tf_op jit(solution)/shard_map/all_gather | solution.py:42
  107.7 242.8 %all-gather.4.cloned.1.call-start = ((), (), s32[]{:S(2)}) async-start(), calls=%async_computation.6 | async-start | bytes 13516800 | tf_op jit(solution)/shard_map/all_gather | solution.py:46
  108.5 357.9 %reduce-scatter.2.cloned.1.call-start = ((), (), s32[]{:S(2)}) async-start(), calls=%async_computation.7 | async-start | bytes 442368 | tf_op jit(solution)/shard_map/reduce_scatter | solution.py:57
  350.6 38.3 %copy-start.4 = (bf16[1280,128]{1,0:T(8,128)(2,1)S(1)}, bf16[1280,128]{1,0:T(8,128)(2,1)}, u32[]{:S(2)}) copy-start(bf16[1280,128]{1,0:T(8,128)(2,1)} %param.14) | copy-start | bytes 983044
  350.6 38.3 %copy-start.5 = (f32[1280]{0:T(1024)S(1)}, f32[1280]{0:T(1024)}, u32[]{:S(2)}) copy-start(f32[1280]{0:T(1024)} %param.13) | copy-start | bytes 15364
  350.6 38.3 %copy-start.6 = (f32[1280]{0:T(1024)S(1)}, f32[1280]{0:T(1024)}, u32[]{:S(2)}) copy-start(f32[1280]{0:T(1024)} %param.12) | copy-start | bytes 15364
  368.5 25.8 %copy-start.7 = (s32[4]{0:T(128)S(1)}, s32[4]{0:T(128)}, u32[]{:S(2)}) copy-start(s32[4]{0:T(128)} %param.17) | copy-start | bytes 52
  388.8 103.2 %copy-start.1 = (bf16[192,5120]{1,0:T(8,128)(2,1)S(1)}, bf16[192,5120]{1,0:T(8,128)(2,1)}, u32[]{:S(2)}) copy-start(bf16[192,5120]{1,0:T(8,128)(2,1)} %param.9) | copy-start | bytes 5898244
  468.3 23.8 %copy-start.2 = (f32[96]{0:T(128)}, f32[96]{0:T(128)S(1)}, u32[]{:S(2)}) copy-start(f32[96]{0:T(128)S(1)} %add_subtract_fusion) | copy-start | bytes 1156
  470.5 17.9 %all-to-all-start.4 = ((f32[32,1,6]{2,1,0:T(1,128)}), f32[32,1,6]{2,1,0:T(1,128)S(1)}, u32[]{:S(2)}, u32[]{:S(2)}) async-start(f32[32,1,6]{2,1,0:T(1,128)} %bitcast.12), calls=%async_computation.5 | async-start | bytes 32768 | tf_op jit(solution)/shard_map/all_to_all | solution.py:112
  491.3 0.7 copy-start.3
Sparse Core Ops, SparseCore 0:
  107.8 140.9 all-gather.5
  250.7 99.8 all-gather.3
  394.4 71.8 reduce-scatter.1
where the time goes:
time: 500 us; the launch traced here: 499 us
  waiting for transfers between devices  188 us (38%)
  blocking collectives  179 us (36%)
  local copies, waits for them, and re-layouts  57.2 us (11%)
  starting transfers between devices  29 us (6%)
  matrix products  24.1 us (5%)
  between operations  14.1 us (3%)
  other arithmetic  7.14 us (1%)
    all_to_all x1, blocking collectives, shards(): lax.all_to_all(send_residual, 'dp', split_axis=0, concat_axis=0, tiled=True)  123 us
    reduce_scatter x1, waiting for transfers between devices, score_rows(): lax.psum_scatter(jnp.dot(normed, head_float, precision=lax.Precision.HIGH...  70.4 us
    all_to_all x1, waiting for transfers between devices, shards(): lax.all_to_all(send_context, 'dp', split_axis=0, concat_axis=0, tiled=True)  59.5 us
    all_gather x1, waiting for transfers between devices, score_rows(): lax.all_gather(out_weight, 'dp', axis=0, tiled=True)  49.1 us
    all_to_all x1, blocking collectives, score_rows(): lax.all_to_all(residual_rows, 'tensor', split_axis=1, concat_axis=0, tile...  35.8 us
    psum x1, blocking collectives, score_rows(): total_sum, total_square = lax.psum((row_sum, row_square), 'tensor')  20.3 us
    dot_general x1, matrix products, score_rows(): jnp.dot(all_context, lax.all_gather(out_weight, 'dp', axis=0, tiled=True)...  18 us
    all_to_all x1, starting transfers between devices, shards(): lax.all_to_all(send_labels, 'dp', split_axis=0, concat_axis=0, tiled=True)  11.1 us
  transfers between devices with their start and end apart: 6, of which 5 were waited for; matrix products, arithmetic and copies ran while one was open for 9% of the time, Pallas kernels for 0%

commit v1 on v0

v1 whole, which is shorter than its diff:
```python
import jax
import jax.numpy as jnp
from jax import lax
from jax.experimental import pallas as pl
from jax.experimental.pallas import tpu as pltpu
from jax.sharding import PartitionSpec as P

MESH = pl.DeviceIdType.MESH
F32 = jnp.float32
BF16 = jnp.bfloat16
EPS = 1e-05
NX, NZ, NDP = 4, 8, 32
ROWS, HALF = 192, 96
KB, NB, CTX, VOCAB = 160, 1280, 5120, 128
LOCAL_WIDTH = 2 * NB
WIDTH = NX * LOCAL_WIDTH
PAIR = 4 * KB


def kernel(
    ctx, res, w, head, gain, bias, info, lens,
    res_out, pk_out, pr_out,
    ctx_all, res_in, transit, w_all, hid, head_all, gain_all, bias_all,
    g_own, g_in, part, part_in, dp_send, dp_in,
    lsem, cs, cr, rs, rr, ws, wr, zs, zr, hs, hr, ns, nr, gs, gr, ps, pr, ds_, dr,
):
    dp = lax.axis_index("dp")
    tensor = lax.axis_index("tensor")
    core = lax.rem(dp, 2)
    z = lax.rem(dp // 2, NZ)
    yl = dp // (2 * NZ)
    x = lax.rem(tensor, NX)
    yh = tensor // NX
    y = yh * 2 + yl

    def x_dev(k):
        return (dp, yh * NX + lax.rem(x + k, NX))

    def y_dev(k):
        to = lax.rem(y + k, 4)
        return ((lax.rem(to, 2) * NZ + z) * 2 + core, (to // 2) * NX + x)

    def z_dev(k):
        return ((yl * NZ + lax.rem(z + k, NZ)) * 2 + core, tensor)

    sibling = (dp + 1 - 2 * core, tensor)
    left, right = lax.rem(x + 3, NX), lax.rem(x + 1, NX)

    def send(src, dst, ssem, rsem, dev):
        copy = pltpu.make_async_remote_copy(
            src_ref=src, dst_ref=dst, send_sem=ssem, recv_sem=rsem,
            device_id=dev, device_id_type=MESH,
        )
        copy.start()
        return copy

    def arrived(ref, sem):
        pltpu.make_async_copy(ref, ref, sem).wait()

    barrier = pltpu.get_barrier_semaphore()

    @pl.loop(1, NDP)
    def _(k):
        pl.semaphore_signal(barrier, inc=1, device_id=(lax.rem(dp + k, NDP), tensor), device_id_type=MESH)

    for k in (1, 2, 3):
        pl.semaphore_signal(barrier, inc=1, device_id=x_dev(k), device_id_type=MESH)
    for other in (yl, 1 - yl):
        pl.semaphore_signal(
            barrier, inc=1, device_id=((other * NZ + z) * 2 + core, (1 - yh) * NX + x), device_id_type=MESH
        )
    pl.semaphore_wait(barrier, NDP - 1 + 5)

    mine = w_all.at[yh, yl, z, core]
    w_out = [send(w, mine, ws.at[k - 1], wr.at[k - 1], y_dev(k)) for k in (1, 2, 3)]
    w_own = pltpu.make_async_copy(w, mine, lsem.at[0])
    w_own.start()

    def ctx_part(ref, part_of):
        return ref.at[pl.ds(part_of * HALF, HALF)]

    c_out = []

    def send_ctx(way, part_of):
        at = way * 2 + part_of
        c_out.append(
            send(
                ctx_part(ctx, part_of), ctx_part(ctx_all.at[x], part_of), cs.at[at], cr.at[at],
                x_dev(1 if way == 0 else 3),
            )
        )

    def columns(block, to):
        return pl.ds(pl.multiple_of((block * NX + to) * NB, NB), NB)

    opposite = lax.rem(x + 2, NX)
    r_out = []
    send_ctx(0, 0)
    send_ctx(1, 1)
    for way in (0, 1):
        for block in (0, 1):
            at = way * 2 + block
            r_out.append(
                send(
                    res.at[pl.ds(way * HALF, HALF), columns(block, opposite)], transit.at[way, block],
                    rs.at[at], rr.at[at], x_dev(1 if way == 0 else 3),
                )
            )
    send_ctx(0, 1)
    send_ctx(1, 0)
    for way in (0, 1):
        for block in (0, 1):
            at = 4 + way * 2 + block
            r_out.append(
                send(
                    res.at[:, columns(block, right if way == 0 else left)], res_in.at[x, block],
                    rs.at[at], rr.at[at], x_dev(1 if way == 0 else 3),
                )
            )
    partner = y_dev(2)
    n_out = [
        send(head, head_all.at[yh], ns.at[0], nr.at[0], partner),
        send(gain, gain_all.at[yh], ns.at[1], nr.at[1], partner),
        send(bias, bias_all.at[yh], ns.at[2], nr.at[2], partner),
    ]
    own = [
        pltpu.make_async_copy(ctx, ctx_all.at[x], lsem.at[1]),
        pltpu.make_async_copy(res.at[:, columns(0, x)], res_in.at[x, 0], lsem.at[2]),
        pltpu.make_async_copy(res.at[:, columns(1, x)], res_in.at[x, 1], lsem.at[3]),
        pltpu.make_async_copy(head, head_all.at[yh], lsem.at[4]),
        pltpu.make_async_copy(gain, gain_all.at[yh], lsem.at[5]),
        pltpu.make_async_copy(bias, bias_all.at[yh], lsem.at[6]),
    ]
    for copy in own:
        copy.start()

    w_own.wait()
    for k in (1, 2, 3):
        wfrom = lax.rem(y + 4 - k, 4)
        arrived(w_all.at[wfrom // 2, lax.rem(wfrom, 2), z, core], wr.at[k - 1])

    h_out, z_out = [], []

    def bundle(at):
        return w_all.at[:, :, at, core]

    def hand(at, slot):
        h_out.append(send(bundle(at), bundle(at), hs.at[slot], hr.at[slot], sibling))

    def pass_on(at, step):
        up, down = at
        if step < 3:
            z_out.append(send(bundle(up), bundle(up), zs.at[step], zr.at[step], z_dev(1)))
            z_out.append(send(bundle(down), bundle(down), zs.at[4 + step], zr.at[4 + step], z_dev(NZ - 1)))
        else:
            z_out.append(send(w_all.at[0, :, up, core], w_all.at[0, :, up, core], zs.at[3], zr.at[3], z_dev(1)))
            z_out.append(
                send(w_all.at[1, :, down, core], w_all.at[1, :, down, core], zs.at[7], zr.at[7], z_dev(NZ - 1))
            )

    def step_in(step):
        below, above = lax.rem(z + NZ - step, NZ), lax.rem(z + step, NZ)
        if step < 4:
            arrived(bundle(below), zr.at[step - 1])
            arrived(bundle(above), zr.at[4 + step - 1])
            pass_on((below, above), step)
            hand(below, 2 * step - 1)
            hand(above, 2 * step)
        else:
            arrived(w_all.at[0, :, below, core], zr.at[3])
            arrived(w_all.at[1, :, below, core], zr.at[7])
            hand(below, 7)

    def handed(step):
        below, above = lax.rem(z + NZ - step, NZ), lax.rem(z + step, NZ)
        if step == 0:
            arrived(w_all.at[:, :, z, 1 - core], hr.at[0])
        elif step < 4:
            arrived(w_all.at[:, :, below, 1 - core], hr.at[2 * step - 1])
            arrived(w_all.at[:, :, above, 1 - core], hr.at[2 * step])
        else:
            arrived(w_all.at[:, :, below, 1 - core], hr.at[7])

    def multiply(pair, first):
        @pl.loop(0, LOCAL_WIDTH // 256)
        def _(n):
            block, at = n // 5, lax.rem(n, 5)
            cols = pl.ds(pl.multiple_of(at * 256, 256), 256)
            total = None
            for low in (0, 1):
                feats = pl.ds(pl.multiple_of((low * 4 + pair) * PAIR, PAIR), PAIR)
                a = ctx_all[:, :, feats].reshape(NX * ROWS, PAIR)
                b = w_all[block, low, pl.ds(pair * 2, 2), :, :, cols].reshape(PAIR, 256)
                term = jnp.dot(a, b, preferred_element_type=F32)
                total = term if total is None else total + term
            if first:
                hid[block, :, cols] = total
            else:
                hid[block, :, cols] += total

    pass_on((z, z), 0)
    hand(z, 0)

    arrived(ctx_part(ctx_all.at[left], 0), cr.at[0])
    c_out.append(
        send(ctx_part(ctx_all.at[left], 0), ctx_part(ctx_all.at[left], 0), cs.at[4], cr.at[4], x_dev(1))
    )
    arrived(ctx_part(ctx_all.at[right], 1), cr.at[3])
    c_out.append(
        send(ctx_part(ctx_all.at[right], 1), ctx_part(ctx_all.at[right], 1), cs.at[5], cr.at[5], x_dev(3))
    )
    step_in(1)

    for way in (0, 1):
        for block in (0, 1):
            arrived(transit.at[way, block], rr.at[way * 2 + block])
        spot = res_in.at[left if way == 0 else right, :, pl.ds(way * HALF, HALF)]
        r_out.append(send(transit.at[way], spot, rs.at[8 + way], rr.at[8 + way], x_dev(1 if way == 0 else 3)))

    own[3].wait()
    own[4].wait()
    own[5].wait()
    arrived(head_all.at[1 - yh], nr.at[0])
    arrived(gain_all.at[1 - yh], nr.at[1])
    arrived(bias_all.at[1 - yh], nr.at[2])
    g_row = jnp.zeros((8, VOCAB), F32)
    for block in (0, 1):
        lhs = jnp.concatenate(
            [
                jnp.broadcast_to(gain_all[block], (4, NB)),
                jnp.broadcast_to(bias_all[block], (4, NB)),
            ],
            axis=0,
        )
        for _ in range(3):
            top = lhs.astype(BF16)
            g_row += jnp.dot(top, head_all[block], preferred_element_type=F32)
            lhs = lhs - top.astype(F32)
    g_own[...] = g_row
    g_out = [send(g_own, g_in.at[k], gs.at[k], gr.at[k], x_dev(k + 1)) for k in range(3)]

    step_in(2)

    own[0].wait()
    arrived(ctx_part(ctx_all.at[left], 1), cr.at[1])
    arrived(ctx_part(ctx_all.at[right], 0), cr.at[2])
    arrived(ctx_part(ctx_all.at[opposite], 0), cr.at[4])
    arrived(ctx_part(ctx_all.at[opposite], 1), cr.at[5])

    base = z // 2
    odd = lax.rem(z, 2)
    handed(0)
    handed(1)
    multiply(base, True)
    step_in(3)
    handed(2)
    multiply(lax.rem(base + 3 + 2 * odd, 4), False)
    handed(3)
    multiply(lax.rem(base + 1 + 2 * odd, 4), False)
    step_in(4)
    handed(4)
    multiply(lax.rem(base + 2, 4), False)

    own[1].wait()
    own[2].wait()
    for way in (0, 1):
        frm = left if way == 0 else right
        for block in (0, 1):
            arrived(res_in.at[frm, block], rr.at[4 + way * 2 + block])
    for way in (0, 1):
        arrived(res_in.at[opposite, :, pl.ds(way * HALF, HALF)], rr.at[8 + way])

    def block_part(k):
        rows_of = lax.rem(x + k + 1, NX)
        at = pl.ds(pl.multiple_of(rows_of * ROWS, ROWS), ROWS)
        row_sum = jnp.zeros((ROWS, 1), F32)
        for block in (0, 1):
            full = hid[block, at] + res_in[rows_of, block].astype(F32)
            hid[block, at] = full
            row_sum += jnp.sum(full, axis=1, keepdims=True)
        mean = row_sum * (1.0 / LOCAL_WIDTH)
        square = jnp.zeros((ROWS, 1), F32)
        product = jnp.zeros((ROWS, VOCAB), F32)
        for block in (0, 1):
            off = hid[block, at] - mean
            square += jnp.sum(off * off, axis=1, keepdims=True)
            scaled = off * gain_all[block]
            top = scaled.astype(BF16)
            rest = (scaled - top.astype(F32)).astype(BF16)
            product += jnp.dot(top, head_all[block], preferred_element_type=F32)
            product += jnp.dot(rest, head_all[block], preferred_element_type=F32)
        lane = lax.broadcasted_iota(jnp.int32, (ROWS, VOCAB), 1)
        part[k, :, :VOCAB] = product
        part[k, :, VOCAB:] = jnp.where(lane == 0, mean, square)

    @pl.loop(0, 3)
    def _(k):
        block_part(k)
        send(part.at[k], part_in.at[k], ps.at[k], pr.at[k], x_dev(k + 1))

    block_part(3)

    label = jnp.transpose(jnp.broadcast_to(info[0:1, :].astype(F32), (VOCAB, 256)))[:ROWS]
    for k in range(3):
        arrived(g_in.at[k], gr.at[k])
        arrived(part_in.at[k], pr.at[k])
    parts = [part[3]] + [part_in[k] for k in range(3)]
    sums = [g_own[...]] + [g_in[k] for k in range(3)]
    means = [p[:, VOCAB : VOCAB + 1] for p in parts]
    squares = [p[:, VOCAB + 1 : VOCAB + 2] for p in parts]
    center = (means[0] + means[1] + means[2] + means[3]) * 0.25
    total_square = squares[0] + squares[1] + squares[2] + squares[3]
    logits = jnp.zeros((ROWS, VOCAB), F32)
    shift = jnp.zeros((1, VOCAB), F32)
    for p, g, m in zip(parts, sums, means):
        away = m - center
        total_square += LOCAL_WIDTH * (away * away)
        logits += p[:, :VOCAB] + away * g[0:1]
        shift += g[4:5]
    logits = logits * lax.rsqrt(total_square * (1.0 / WIDTH) + EPS) + shift
    largest = jnp.max(logits, axis=1, keepdims=True)
    log_total = largest + jnp.log(jnp.sum(jnp.exp(logits - largest), axis=1, keepdims=True))
    token = lax.broadcasted_iota(jnp.int32, (ROWS, VOCAB), 1).astype(F32)
    picked = jnp.sum(jnp.where(token == label, logits, 0.0), axis=1, keepdims=True)
    score = jnp.broadcast_to(picked - log_total, (ROWS, VOCAB))
    score_rows = jnp.transpose(jnp.concatenate([score, jnp.zeros((256 - ROWS, VOCAB), F32)], axis=0))

    group = info[1:2, :]
    place = info[2:3, :]
    lhs = jnp.where(lax.broadcasted_iota(jnp.int32, (NDP, 256), 0) == group, score_rows[:NDP], 0.0)
    spots = jnp.where(lax.broadcasted_iota(jnp.int32, (VOCAB, 256), 0) == place, 1.0, 0.0).astype(BF16)
    packed = jnp.zeros((NDP, VOCAB), F32)
    for _ in range(3):
        top = lhs.astype(BF16)
        packed += lax.dot_general(top, spots, (((1,), (1,)), ((), ())), preferred_element_type=F32)
        lhs = lhs - top.astype(F32)
    dp_send[...] = packed.reshape(NDP, 1, VOCAB)

    @pl.loop(1, NDP)
    def _(k):
        to = lax.rem(dp + k, NDP)
        send(dp_send.at[to], dp_in.at[k - 1], ds_.at[0], dr.at[0], (to, tensor))

    live_score = jnp.where(group >= 0, score_rows[0:1], 0.0)
    res_out[...] = live_score[:, :ROWS]
    at_row = lax.broadcasted_iota(jnp.int32, (1, 256), 1)
    lane = lax.broadcasted_iota(jnp.int32, (1, VOCAB), 1)
    begin = jnp.int32(0)
    proteins = jnp.zeros((1, VOCAB), F32)
    for i in range(4):
        length = lens[i]
        end = begin + length
        inside = jnp.where((at_row >= begin) & (at_row < end), live_score, 0.0)
        one = jnp.sum(inside, axis=1, keepdims=True) / jnp.broadcast_to(
            jnp.maximum(length, 1).astype(F32), (1, 1)
        )
        proteins = jnp.where(lane == i, one, proteins)
        begin = end
    pr_out[...] = proteins[:, :4]

    for copy in w_out + c_out + r_out + n_out + z_out + h_out + g_out:
        copy.wait_send()
    for k in range(3):
        arrived(part.at[k], ps.at[k])
    arrived(dp_in, dr.at[0])
    arrived(dp_in, ds_.at[0])
    packed_row = dp_send[dp] + jnp.sum(dp_in[...], axis=0)
    pk_out[...] = packed_row[:, :HALF]


def shards(context, residual, out_weight, norm_gain, norm_bias, head_weight, targets, packing, lengths):
    info = jnp.pad(
        jnp.concatenate([targets[None], packing], axis=0), ((0, 5), (0, 256 - ROWS)), constant_values=-1
    )
    any_ = pl.BlockSpec(memory_space=pl.ANY)
    vmem = pl.BlockSpec(memory_space=pltpu.VMEM)
    dma = pltpu.SemaphoreType.DMA
    scores, packed, proteins = pl.pallas_call(
        kernel,
        out_shape=(
            jax.ShapeDtypeStruct((1, ROWS), F32),
            jax.ShapeDtypeStruct((1, HALF), F32),
            jax.ShapeDtypeStruct((1, 4), F32),
        ),
        in_specs=[any_] * 6 + [vmem, pl.BlockSpec(memory_space=pltpu.SMEM)],
        out_specs=(vmem, vmem, vmem),
        scratch_shapes=[
            pltpu.VMEM((NX, ROWS, CTX), BF16),
            pltpu.VMEM((NX, 2, ROWS, NB), BF16),
            pltpu.VMEM((2, 2, HALF, NB), BF16),
            pltpu.VMEM((2, 2, NZ, 2, KB, NB), BF16),
            pltpu.VMEM((2, NX * ROWS, NB), F32),
            pltpu.VMEM((2, NB, VOCAB), BF16),
            pltpu.VMEM((2, 1, NB), F32),
            pltpu.VMEM((2, 1, NB), F32),
            pltpu.VMEM((8, VOCAB), F32),
            pltpu.VMEM((3, 8, VOCAB), F32),
            pltpu.VMEM((4, ROWS, 2 * VOCAB), F32),
            pltpu.VMEM((3, ROWS, 2 * VOCAB), F32),
            pltpu.VMEM((NDP, 1, VOCAB), F32),
            pltpu.VMEM((NDP - 1, 1, VOCAB), F32),
            dma((7,)),
            dma((6,)), dma((6,)),
            dma((10,)), dma((10,)),
            dma((3,)), dma((3,)),
            dma((8,)), dma((8,)),
            dma((8,)), dma((8,)),
            dma((3,)), dma((3,)),
            dma((3,)), dma((3,)),
            dma((3,)), dma((3,)),
            dma((1,)), dma((1,)),
        ],
        compiler_params=pltpu.CompilerParams(
            collective_id=0, has_side_effects=True, vmem_limit_bytes=60 * 2**20
        ),
    )(
        context, residual, out_weight, head_weight,
        norm_gain.reshape(1, NB), norm_bias.reshape(1, NB), info, lengths,
    )
    return scores.reshape(ROWS), packed.reshape(HALF), proteins.reshape(4)


def solution(mesh):
    placed = (
        P(("dp", "tensor"), None),
        P(("dp", "tensor"), None),
        P("dp", "tensor"),
        P("tensor"),
        P("tensor"),
        P("tensor", None),
        P(("dp", "tensor")),
        P(None, ("dp", "tensor")),
        P(("dp", "tensor")),
    )
    rows = P(("dp", "tensor"))
    return jax.shard_map(shards, mesh=mesh, in_specs=placed, out_specs=(rows, rows, rows), check_vma=False)
```

time: 500 us -> 195 us (0.39)
  waiting for transfers between devices: 188 us -> 0 us
  Pallas kernels: 0 us -> 187 us
  blocking collectives: 179 us -> 0 us
  local copies, waits for them, and re-layouts: 57.2 us -> 6.59 us
  starting transfers between devices: 29 us -> 0 us
  matrix products: 24.1 us -> 0 us
  between operations: 14.1 us -> 0.64 us
  other arithmetic: 7.14 us -> 0.71 us
    pallas_call x0 -> x1, Pallas kernels: none -> 187 us  [shards(): pl.pallas_call(kernel, out_shape=(jax.ShapeDtypeStruct((1, ROWS), F32), j...]
    all_to_all x2 -> x0, blocking collectives: 158 us -> none  [the longest x1 123 us: shards(): lax.all_to_all(send_residual, 'dp', split_axis=0, concat_axis=0, tiled=True)]
    reduce_scatter x1 -> x0, waiting for transfers between devices: 70.4 us -> none  [score_rows(): lax.psum_scatter(jnp.dot(normed, head_float, precision=lax.Precision.HIGH...]
    all_to_all x3 -> x0, waiting for transfers between devices: 68.1 us -> none  [the longest x1 59.5 us: shards(): lax.all_to_all(send_context, 'dp', split_axis=0, concat_axis=0, tiled=True)]
    all_gather x2 -> x0, waiting for transfers between devices: 49.1 us -> none  [the longest x1 49.1 us: score_rows(): lax.all_gather(out_weight, 'dp', axis=0, tiled=True)]
    gather x10 -> x0, local copies, waits for them, and re-layouts: 30.4 us -> none  [the longest x1 11.1 us: shards(): residual[safe_index].reshape(group_count, slot_width, model_width)]
    all_to_all x3 -> x0, starting transfers between devices: 28.7 us -> none  [the longest x1 11.1 us: shards(): lax.all_to_all(send_labels, 'dp', split_axis=0, concat_axis=0, tiled=True)]
    dot_general x3 -> x0, matrix products: 24.1 us -> none  [the longest x1 18 us: score_rows(): jnp.dot(all_context, lax.all_gather(out_weight, 'dp', axis=0, tiled=True)...]
  transfers between devices with their start and end apart: 6 -> 0, of which waited for: 5 -> 0; matrix products, arithmetic and copies ran while one was open for 9% -> 0% of each run, Pallas kernels for 0% -> 0%
where the time goes in v1:
time: 195 us
  Pallas kernels  187 us (96%)
  local copies, waits for them, and re-layouts  6.59 us (3%)
    pallas_call x1, Pallas kernels, shards(): pl.pallas_call(kernel, out_shape=(jax.ShapeDtypeStruct((1, ROWS), F32), j...  187 us

profile of v1, /device:TPU:1, one launch (start us, length us, event | category | flops | bytes accessed | tf_op | source)
XLA Modules:
  0.0 194.9 jit_solution(17876333417197776252)
XLA Ops:
  0.6 0.7 pad_add_fusion
  1.3 0.6 pad.4.info
  1.9 1.3 reshape.21.gain
  3.2 1.3 reshape.22.bias
  4.5 186.9 %shard_map.112 = (f32[1,192]{1,0:T(1,128)}, f32[1,96]{1,0:T(1,128)}, f32[1,4]{1,0:T(1,128)}) custom-call(bf16[192,5120]{1,0:T(8,128)(2,1)} %ctx.1, bf16[192,10240]{1,0:T(8,128)(2,1)} %res.1, bf16[160,1280]{1,0:T(8,128)(2,1)} %w.1, bf16[1280,128]{1,0:T(8,128)(2,1)} %head.1, f32[1,1280]{1,0:T(1,128)} %reshape.21.gain, f32[1,1280]{1,0:T(1,128)} %reshape.22.bias, ...), custom_call_target="tpu_custom_call" | custom-call | tf_op jit(solution)/shard_map/pallas_call | solution.py:378
  191.4 1.2 copy.15
  192.6 1.1 copy.16
  193.7 1.1 copy.17

commit v2 on v1

--- a/solution.py
+++ b/solution.py
@@ -14,15 +14,18 @@
 KB, NB, CTX, VOCAB = 160, 1280, 5120, 128
 LOCAL_WIDTH = 2 * NB
 WIDTH = NX * LOCAL_WIDTH
+RA = 64
+RB = KB - RA
+RH = RB // 2
 PAIR = 4 * KB
 
 
 def kernel(
-    ctx, res, w, head, gain, bias, info, lens,
-    res_out, pk_out, pr_out,
+    ctx, res, w, head, gain, bias, targets, packing, lens,
+    out,
     ctx_all, res_in, transit, w_all, hid, head_all, gain_all, bias_all,
-    g_own, g_in, part, part_in, dp_send, dp_in,
-    lsem, cs, cr, rs, rr, ws, wr, zs, zr, hs, hr, ns, nr, gs, gr, ps, pr, ds_, dr,
+    g_own, g_in, part, part_in, info, dp_send, dp_in,
+    lsem, cs, cr, rs, rr, ws, wr, zs, zr, bs, br, us, ur, os, or_, hs, hr, ns, nr, gs, gr, ps, pr, ds_, dr,
 ):
     dp = lax.axis_index("dp")
     tensor = lax.axis_index("tensor")
@@ -71,9 +74,19 @@
         )
     pl.semaphore_wait(barrier, NDP - 1 + 5)
 
-    mine = w_all.at[yh, yl, z, core]
-    w_out = [send(w, mine, ws.at[k - 1], wr.at[k - 1], y_dev(k)) for k in (1, 2, 3)]
-    w_own = pltpu.make_async_copy(w, mine, lsem.at[0])
+    first, second = pl.ds(0, RA), pl.ds(RA, RB)
+    upper, lower = pl.ds(RA, RH), pl.ds(RA + RH, RH)
+
+    def piece(of_y, at, rows):
+        return w_all.at[of_y // 2, lax.rem(of_y, 2), at, core, rows]
+
+    b_out = []
+    w_out = [send(w.at[first], piece(y, z, first), ws.at[k - 1], wr.at[k - 1], y_dev(k)) for k in (1, 2, 3)]
+    for way, to in ((0, z_dev(1)), (1, z_dev(NZ - 1))):
+        b_out.append(send(w.at[second], piece(y, z, second), bs.at[4 * way], br.at[4 * way], to))
+    for way, to in ((0, y_dev(1)), (1, y_dev(3))):
+        b_out.append(send(w.at[second], piece(y, z, second), us.at[way], ur.at[way], to))
+    w_own = pltpu.make_async_copy(w, w_all.at[yh, yl, z, core], lsem.at[0])
     w_own.start()
 
     def ctx_part(ref, part_of):
@@ -120,68 +133,95 @@
     partner = y_dev(2)
     n_out = [
         send(head, head_all.at[yh], ns.at[0], nr.at[0], partner),
-        send(gain, gain_all.at[yh], ns.at[1], nr.at[1], partner),
-        send(bias, bias_all.at[yh], ns.at[2], nr.at[2], partner),
+        send(gain, gain_all.at[yh, 0], ns.at[1], nr.at[1], partner),
+        send(bias, bias_all.at[yh, 0], ns.at[2], nr.at[2], partner),
     ]
     own = [
         pltpu.make_async_copy(ctx, ctx_all.at[x], lsem.at[1]),
         pltpu.make_async_copy(res.at[:, columns(0, x)], res_in.at[x, 0], lsem.at[2]),
         pltpu.make_async_copy(res.at[:, columns(1, x)], res_in.at[x, 1], lsem.at[3]),
         pltpu.make_async_copy(head, head_all.at[yh], lsem.at[4]),
-        pltpu.make_async_copy(gain, gain_all.at[yh], lsem.at[5]),
-        pltpu.make_async_copy(bias, bias_all.at[yh], lsem.at[6]),
+        pltpu.make_async_copy(gain, gain_all.at[yh, 0], lsem.at[5]),
+        pltpu.make_async_copy(bias, bias_all.at[yh, 0], lsem.at[6]),
     ]
     for copy in own:
         copy.start()
 
-    w_own.wait()
-    for k in (1, 2, 3):
-        wfrom = lax.rem(y + 4 - k, 4)
-        arrived(w_all.at[wfrom // 2, lax.rem(wfrom, 2), z, core], wr.at[k - 1])
-
     h_out, z_out = [], []
 
+    def below(step):
+        return lax.rem(z + NZ - step, NZ)
+
+    def above(step):
+        return lax.rem(z + step, NZ)
+
+    def spots(step):
+        if step == 0:
+            return [(z, 0)]
+        if step == 4:
+            return [(below(4), 7)]
+        return [(below(step), 2 * step - 1), (above(step), 2 * step)]
+
     def bundle(at):
-        return w_all.at[:, :, at, core]
-
-    def hand(at, slot):
-        h_out.append(send(bundle(at), bundle(at), hs.at[slot], hr.at[slot], sibling))
-
-    def pass_on(at, step):
-        up, down = at
+        return w_all.at[:, :, at, core, first]
+
+    def a_in(step):
+        if step == 0:
+            w_own.wait()
+            for k in (1, 2, 3):
+                arrived(piece(lax.rem(y + 4 - k, 4), z, first), wr.at[k - 1])
+        elif step < 4:
+            arrived(bundle(below(step)), zr.at[step - 1])
+            arrived(bundle(above(step)), zr.at[4 + step - 1])
+        else:
+            arrived(w_all.at[0, :, below(4), core, first], zr.at[3])
+            arrived(w_all.at[1, :, below(4), core, first], zr.at[7])
         if step < 3:
-            z_out.append(send(bundle(up), bundle(up), zs.at[step], zr.at[step], z_dev(1)))
-            z_out.append(send(bundle(down), bundle(down), zs.at[4 + step], zr.at[4 + step], z_dev(NZ - 1)))
+            up, down = bundle(below(step)), bundle(above(step))
+        elif step == 3:
+            up, down = w_all.at[0, :, below(3), core, first], w_all.at[1, :, above(3), core, first]
         else:
-            z_out.append(send(w_all.at[0, :, up, core], w_all.at[0, :, up, core], zs.at[3], zr.at[3], z_dev(1)))
-            z_out.append(
-                send(w_all.at[1, :, down, core], w_all.at[1, :, down, core], zs.at[7], zr.at[7], z_dev(NZ - 1))
-            )
-
-    def step_in(step):
-        below, above = lax.rem(z + NZ - step, NZ), lax.rem(z + step, NZ)
+            return
+        z_out.append(send(up, up, zs.at[step], zr.at[step], z_dev(1)))
+        z_out.append(send(down, down, zs.at[4 + step], zr.at[4 + step], z_dev(NZ - 1)))
+
+    def b_in(step):
         if step < 4:
-            arrived(bundle(below), zr.at[step - 1])
-            arrived(bundle(above), zr.at[4 + step - 1])
-            pass_on((below, above), step)
-            hand(below, 2 * step - 1)
-            hand(above, 2 * step)
+            arrived(piece(y, below(step), second), br.at[step - 1])
+            arrived(piece(y, above(step), second), br.at[4 + step - 1])
+            up_rows, down_rows = (second, second) if step < 3 else (upper, lower)
+            up, down = piece(y, below(step), up_rows), piece(y, above(step), down_rows)
+            b_out.append(send(up, up, bs.at[step], br.at[step], z_dev(1)))
+            b_out.append(send(down, down, bs.at[4 + step], br.at[4 + step], z_dev(NZ - 1)))
         else:
-            arrived(w_all.at[0, :, below, core], zr.at[3])
-            arrived(w_all.at[1, :, below, core], zr.at[7])
-            hand(below, 7)
+            arrived(piece(y, below(4), upper), br.at[3])
+            arrived(piece(y, below(4), lower), br.at[7])
+        for at, number in spots(step):
+            spot = piece(y, at, second)
+            b_out.append(send(spot, spot, us.at[2 * number], ur.at[2 * number], y_dev(1)))
+            b_out.append(send(spot, spot, us.at[2 * number + 1], ur.at[2 * number + 1], y_dev(3)))
+
+    def relay(step):
+        for at, number in spots(step):
+            for way, frm, rows in ((0, lax.rem(y + 3, 4), upper), (1, lax.rem(y + 1, 4), lower)):
+                arrived(piece(frm, at, second), ur.at[2 * number + way])
+                spot = piece(frm, at, rows)
+                b_out.append(
+                    send(spot, spot, os.at[2 * number + way], or_.at[2 * number + way], y_dev(1 if way == 0 else 3))
+                )
+
+    def hand(step):
+        for at, number in spots(step):
+            for way, rows in ((0, upper), (1, lower)):
+                arrived(piece(lax.rem(y + 2, 4), at, rows), or_.at[2 * number + way])
+            whole = w_all.at[:, :, at, core]
+            h_out.append(send(whole, whole, hs.at[number], hr.at[number], sibling))
 
     def handed(step):
-        below, above = lax.rem(z + NZ - step, NZ), lax.rem(z + step, NZ)
-        if step == 0:
-            arrived(w_all.at[:, :, z, 1 - core], hr.at[0])
-        elif step < 4:
-            arrived(w_all.at[:, :, below, 1 - core], hr.at[2 * step - 1])
-            arrived(w_all.at[:, :, above, 1 - core], hr.at[2 * step])
-        else:
-            arrived(w_all.at[:, :, below, 1 - core], hr.at[7])
-
-    def multiply(pair, first):
+        for at, number in spots(step):
+            arrived(w_all.at[:, :, at, 1 - core], hr.at[number])
+
+    def multiply(pair, start):
         @pl.loop(0, LOCAL_WIDTH // 256)
         def _(n):
             block, at = n // 5, lax.rem(n, 5)
@@ -193,13 +233,14 @@
                 b = w_all[block, low, pl.ds(pair * 2, 2), :, :, cols].reshape(PAIR, 256)
                 term = jnp.dot(a, b, preferred_element_type=F32)
                 total = term if total is None else total + term
-            if first:
+            if start:
                 hid[block, :, cols] = total
             else:
                 hid[block, :, cols] += total
 
-    pass_on((z, z), 0)
-    hand(z, 0)
+    a_in(0)
+    b_in(1)
+    relay(0)
 
     arrived(ctx_part(ctx_all.at[left], 0), cr.at[0])
     c_out.append(
@@ -209,7 +250,10 @@
     c_out.append(
         send(ctx_part(ctx_all.at[right], 1), ctx_part(ctx_all.at[right], 1), cs.at[5], cr.at[5], x_dev(3))
     )
-    step_in(1)
+    a_in(1)
+    b_in(2)
+    relay(1)
+    hand(0)
 
     for way in (0, 1):
         for block in (0, 1):
@@ -221,8 +265,8 @@
     own[4].wait()
     own[5].wait()
     arrived(head_all.at[1 - yh], nr.at[0])
-    arrived(gain_all.at[1 - yh], nr.at[1])
-    arrived(bias_all.at[1 - yh], nr.at[2])
+    arrived(gain_all.at[1 - yh, 0], nr.at[1])
+    arrived(bias_all.at[1 - yh, 0], nr.at[2])
     g_row = jnp.zeros((8, VOCAB), F32)
     for block in (0, 1):
         lhs = jnp.concatenate(
@@ -239,7 +283,10 @@
     g_own[...] = g_row
     g_out = [send(g_own, g_in.at[k], gs.at[k], gr.at[k], x_dev(k + 1)) for k in range(3)]
 
-    step_in(2)
+    a_in(2)
+    b_in(3)
+    relay(2)
+    hand(1)
 
     own[0].wait()
     arrived(ctx_part(ctx_all.at[left], 1), cr.at[1])
@@ -252,12 +299,18 @@
     handed(0)
     handed(1)
     multiply(base, True)
-    step_in(3)
+    a_in(3)
+    b_in(4)
+    relay(3)
+    hand(2)
     handed(2)
     multiply(lax.rem(base + 3 + 2 * odd, 4), False)
+    a_in(4)
+    relay(4)
+    hand(3)
     handed(3)
     multiply(lax.rem(base + 1 + 2 * odd, 4), False)
-    step_in(4)
+    hand(4)
     handed(4)
     multiply(lax.rem(base + 2, 4), False)
 
@@ -290,8 +343,13 @@
             product += jnp.dot(top, head_all[block], preferred_element_type=F32)
             product += jnp.dot(rest, head_all[block], preferred_element_type=F32)
         lane = lax.broadcasted_iota(jnp.int32, (ROWS, VOCAB), 1)
-        part[k, :, :VOCAB] = product
-        part[k, :, VOCAB:] = jnp.where(lane == 0, mean, square)
+        both = jnp.concatenate(
+            [jnp.where(lane == 0, mean, square), jnp.zeros((256 - ROWS, VOCAB), F32)], axis=0
+        )
+        both = jnp.transpose(both)[:8]
+        part[k, :ROWS] = product
+        part[k, ROWS : ROWS + 8] = both[:, :VOCAB]
+        part[k, ROWS + 8 :] = both[:, VOCAB:]
 
     @pl.loop(0, 3)
     def _(k):
@@ -300,24 +358,29 @@
 
     block_part(3)
 
+    info[...] = jnp.full((8, 256), -1, jnp.int32)
+    info[0:1, :ROWS] = targets[...].reshape(1, ROWS)
+    info[1:3, :ROWS] = packing[...]
     label = jnp.transpose(jnp.broadcast_to(info[0:1, :].astype(F32), (VOCAB, 256)))[:ROWS]
     for k in range(3):
         arrived(g_in.at[k], gr.at[k])
         arrived(part_in.at[k], pr.at[k])
     parts = [part[3]] + [part_in[k] for k in range(3)]
     sums = [g_own[...]] + [g_in[k] for k in range(3)]
-    means = [p[:, VOCAB : VOCAB + 1] for p in parts]
-    squares = [p[:, VOCAB + 1 : VOCAB + 2] for p in parts]
-    center = (means[0] + means[1] + means[2] + means[3]) * 0.25
-    total_square = squares[0] + squares[1] + squares[2] + squares[3]
+    stats = [jnp.concatenate([p[ROWS : ROWS + 8], p[ROWS + 8 :]], axis=1) for p in parts]
+    center = (stats[0][0:1] + stats[1][0:1] + stats[2][0:1] + stats[3][0:1]) * 0.25
+    total_square = stats[0][1:2] + stats[1][1:2] + stats[2][1:2] + stats[3][1:2]
+    away = [st[0:1] - center for st in stats]
+    for a in away:
+        total_square += LOCAL_WIDTH * (a * a)
+    inverse = lax.rsqrt(total_square * (1.0 / WIDTH) + EPS)
+    by_row = jnp.transpose(jnp.concatenate([inverse, *away, jnp.zeros((VOCAB - 5, 256), F32)], axis=0))[:ROWS]
     logits = jnp.zeros((ROWS, VOCAB), F32)
     shift = jnp.zeros((1, VOCAB), F32)
-    for p, g, m in zip(parts, sums, means):
-        away = m - center
-        total_square += LOCAL_WIDTH * (away * away)
-        logits += p[:, :VOCAB] + away * g[0:1]
-        shift += g[4:5]
-    logits = logits * lax.rsqrt(total_square * (1.0 / WIDTH) + EPS) + shift
+    for i in range(4):
+        logits += parts[i][:ROWS] + by_row[:, i + 1 : i + 2] * sums[i][0:1]
+        shift += sums[i][4:5]
+    logits = logits * by_row[:, 0:1] + shift
     largest = jnp.max(logits, axis=1, keepdims=True)
     log_total = largest + jnp.log(jnp.sum(jnp.exp(logits - largest), axis=1, keepdims=True))
     token = lax.broadcasted_iota(jnp.int32, (ROWS, VOCAB), 1).astype(F32)
@@ -328,11 +391,11 @@
     group = info[1:2, :]
     place = info[2:3, :]
     lhs = jnp.where(lax.broadcasted_iota(jnp.int32, (NDP, 256), 0) == group, score_rows[:NDP], 0.0)
-    spots = jnp.where(lax.broadcasted_iota(jnp.int32, (VOCAB, 256), 0) == place, 1.0, 0.0).astype(BF16)
+    chosen = jnp.where(lax.broadcasted_iota(jnp.int32, (VOCAB, 256), 0) == place, 1.0, 0.0).astype(BF16)
     packed = jnp.zeros((NDP, VOCAB), F32)
     for _ in range(3):
         top = lhs.astype(BF16)
-        packed += lax.dot_general(top, spots, (((1,), (1,)), ((), ())), preferred_element_type=F32)
+        packed += lax.dot_general(top, chosen, (((1,), (1,)), ((), ())), preferred_element_type=F32)
         lhs = lhs - top.astype(F32)
     dp_send[...] = packed.reshape(NDP, 1, VOCAB)
 
@@ -342,7 +405,7 @@
         send(dp_send.at[to], dp_in.at[k - 1], ds_.at[0], dr.at[0], (to, tensor))
 
     live_score = jnp.where(group >= 0, score_rows[0:1], 0.0)
-    res_out[...] = live_score[:, :ROWS]
+    out[0:1] = live_score
     at_row = lax.broadcasted_iota(jnp.int32, (1, 256), 1)
     lane = lax.broadcasted_iota(jnp.int32, (1, VOCAB), 1)
     begin = jnp.int32(0)
@@ -356,34 +419,27 @@
         )
         proteins = jnp.where(lane == i, one, proteins)
         begin = end
-    pr_out[...] = proteins[:, :4]
-
-    for copy in w_out + c_out + r_out + n_out + z_out + h_out + g_out:
+    out[2:3, :VOCAB] = proteins
+
+    for copy in w_out + c_out + r_out + n_out + z_out + b_out + h_out + g_out:
         copy.wait_send()
     for k in range(3):
         arrived(part.at[k], ps.at[k])
     arrived(dp_in, dr.at[0])
     arrived(dp_in, ds_.at[0])
     packed_row = dp_send[dp] + jnp.sum(dp_in[...], axis=0)
-    pk_out[...] = packed_row[:, :HALF]
+    out[1:2, :VOCAB] = packed_row
 
 
 def shards(context, residual, out_weight, norm_gain, norm_bias, head_weight, targets, packing, lengths):
-    info = jnp.pad(
-        jnp.concatenate([targets[None], packing], axis=0), ((0, 5), (0, 256 - ROWS)), constant_values=-1
-    )
     any_ = pl.BlockSpec(memory_space=pl.ANY)
     vmem = pl.BlockSpec(memory_space=pltpu.VMEM)
     dma = pltpu.SemaphoreType.DMA
-    scores, packed, proteins = pl.pallas_call(
+    rows = pl.pallas_call(
         kernel,
-        out_shape=(
-            jax.ShapeDtypeStruct((1, ROWS), F32),
-            jax.ShapeDtypeStruct((1, HALF), F32),
-            jax.ShapeDtypeStruct((1, 4), F32),
-        ),
-        in_specs=[any_] * 6 + [vmem, pl.BlockSpec(memory_space=pltpu.SMEM)],
-        out_specs=(vmem, vmem, vmem),
+        out_shape=jax.ShapeDtypeStruct((8, 256), F32),
+        in_specs=[any_] * 6 + [vmem, vmem, pl.BlockSpec(memory_space=pltpu.SMEM)],
+        out_specs=vmem,
         scratch_shapes=[
             pltpu.VMEM((NX, ROWS, CTX), BF16),
             pltpu.VMEM((NX, 2, ROWS, NB), BF16),
@@ -395,8 +451,9 @@
             pltpu.VMEM((2, 1, NB), F32),
             pltpu.VMEM((8, VOCAB), F32),
             pltpu.VMEM((3, 8, VOCAB), F32),
-            pltpu.VMEM((4, ROWS, 2 * VOCAB), F32),
-            pltpu.VMEM((3, ROWS, 2 * VOCAB), F32),
+            pltpu.VMEM((4, ROWS + 16, VOCAB), F32),
+            pltpu.VMEM((3, ROWS + 16, VOCAB), F32),
+            pltpu.VMEM((8, 256), jnp.int32),
             pltpu.VMEM((NDP, 1, VOCAB), F32),
             pltpu.VMEM((NDP - 1, 1, VOCAB), F32),
             dma((7,)),
@@ -404,6 +461,9 @@
             dma((10,)), dma((10,)),
             dma((3,)), dma((3,)),
             dma((8,)), dma((8,)),
+            dma((8,)), dma((8,)),
+            dma((16,)), dma((16,)),
+            dma((16,)), dma((16,)),
             dma((8,)), dma((8,)),
             dma((3,)), dma((3,)),
             dma((3,)), dma((3,)),
@@ -415,9 +475,9 @@
         ),
     )(
         context, residual, out_weight, head_weight,
-        norm_gain.reshape(1, NB), norm_bias.reshape(1, NB), info, lengths,
+        norm_gain, norm_bias, targets, packing, lengths,
     )
-    return scores.reshape(ROWS), packed.reshape(HALF), proteins.reshape(4)
+    return rows[0, :ROWS], rows[1, :HALF], rows[2, :4]
 
 
 def solution(mesh):

time: 195 us -> 174 us (0.89)
  Pallas kernels: 187 us -> 169 us
  local copies, waits for them, and re-layouts: 6.59 us -> 3.65 us
    pallas_call x1, Pallas kernels: 187 us -> 169 us  [shards(): pl.pallas_call(kernel, out_shape=jax.ShapeDtypeStruct((8, 256), F32), in_...]
    unnamed x3 -> x0, local copies, waits for them, and re-layouts: 3.42 us -> none
    reshape x2 -> x0, local copies, waits for them, and re-layouts: 2.58 us -> none  [the longest x1 1.29 us: shards(): norm_bias.reshape(1, NB)]
    squeeze x0 -> x2, local copies, waits for them, and re-layouts: none -> 2.39 us  [shards(): return (rows[0, :ROWS], rows[1, :HALF], rows[2, :4])]
where the time goes in v2:
time: 174 us
  Pallas kernels  169 us (97%)
  local copies, waits for them, and re-layouts  3.65 us (2%)
    pallas_call x1, Pallas kernels, shards(): pl.pallas_call(kernel, out_shape=jax.ShapeDtypeStruct((8, 256), F32), in_...  169 us

profile of v2, /device:TPU:1, one launch (start us, length us, event | category | flops | bytes accessed | tf_op | source)
XLA Modules:
  0.0 173.5 jit_solution(17598929607344823436)
XLA Ops:
  0.6 169.2 %shard_map.112 = f32[8,256]{1,0:T(8,128)} custom-call(bf16[192,5120]{1,0:T(8,128)(2,1)} %ctx.1, bf16[192,10240]{1,0:T(8,128)(2,1)} %res.1, bf16[160,1280]{1,0:T(8,128)(2,1)} %w.1, bf16[1280,128]{1,0:T(8,128)(2,1)} %head.1, f32[1280]{0:T(1024)} %gain.1, f32[1280]{0:T(1024)} %bias.1, s32[192]{0:T(256)} %targets.1, s32[2,192]{1,0:T(2,128)} %packing.1, s32[4]{0:T(128)} %lens.1), custom_call_target="tpu_custom_call" | custom-call | tf_op jit(solution)/shard_map/pallas_call | solution.py:438
  169.9 1.2 slice_bitcast_fusion
  171.1 1.2 slice_bitcast_fusion.1
  172.3 1.3 slice.9

commit v3 on v2

--- a/solution.py
+++ b/solution.py
@@ -61,18 +61,9 @@
         pltpu.make_async_copy(ref, ref, sem).wait()
 
     barrier = pltpu.get_barrier_semaphore()
-
-    @pl.loop(1, NDP)
-    def _(k):
-        pl.semaphore_signal(barrier, inc=1, device_id=(lax.rem(dp + k, NDP), tensor), device_id_type=MESH)
-
-    for k in (1, 2, 3):
-        pl.semaphore_signal(barrier, inc=1, device_id=x_dev(k), device_id_type=MESH)
-    for other in (yl, 1 - yl):
-        pl.semaphore_signal(
-            barrier, inc=1, device_id=((other * NZ + z) * 2 + core, (1 - yh) * NX + x), device_id_type=MESH
-        )
-    pl.semaphore_wait(barrier, NDP - 1 + 5)
+    for dev in [x_dev(k) for k in (1, 2, 3)] + [y_dev(k) for k in (1, 2, 3)] + [z_dev(1), z_dev(NZ - 1), sibling]:
+        pl.semaphore_signal(barrier, inc=1, device_id=dev, device_id_type=MESH)
+    pl.semaphore_wait(barrier, 9)
 
     first, second = pl.ds(0, RA), pl.ds(RA, RB)
     upper, lower = pl.ds(RA, RH), pl.ds(RA + RH, RH)
@@ -110,26 +101,38 @@
     r_out = []
     send_ctx(0, 0)
     send_ctx(1, 1)
-    for way in (0, 1):
-        for block in (0, 1):
-            at = way * 2 + block
-            r_out.append(
-                send(
-                    res.at[pl.ds(way * HALF, HALF), columns(block, opposite)], transit.at[way, block],
-                    rs.at[at], rr.at[at], x_dev(1 if way == 0 else 3),
-                )
-            )
     send_ctx(0, 1)
     send_ctx(1, 0)
-    for way in (0, 1):
-        for block in (0, 1):
-            at = 4 + way * 2 + block
-            r_out.append(
-                send(
-                    res.at[:, columns(block, right if way == 0 else left)], res_in.at[x, block],
-                    rs.at[at], rr.at[at], x_dev(1 if way == 0 else 3),
+
+    def res_far():
+        for way in (0, 1):
+            for block in (0, 1):
+                at = way * 2 + block
+                r_out.append(
+                    send(
+                        res.at[pl.ds(way * HALF, HALF), columns(block, opposite)], transit.at[way, block],
+                        rs.at[at], rr.at[at], x_dev(1 if way == 0 else 3),
+                    )
                 )
-            )
+
+    def res_near():
+        for way in (0, 1):
+            for block in (0, 1):
+                at = 4 + way * 2 + block
+                r_out.append(
+                    send(
+                        res.at[:, columns(block, right if way == 0 else left)], res_in.at[x, block],
+                        rs.at[at], rr.at[at], x_dev(1 if way == 0 else 3),
+                    )
+                )
+
+    def res_relay():
+        for way in (0, 1):
+            for block in (0, 1):
+                arrived(transit.at[way, block], rr.at[way * 2 + block])
+            spot = res_in.at[left if way == 0 else right, :, pl.ds(way * HALF, HALF)]
+            r_out.append(send(transit.at[way], spot, rs.at[8 + way], rr.at[8 + way], x_dev(1 if way == 0 else 3)))
+
     partner = y_dev(2)
     n_out = [
         send(head, head_all.at[yh], ns.at[0], nr.at[0], partner),
@@ -226,13 +229,17 @@
         def _(n):
             block, at = n // 5, lax.rem(n, 5)
             cols = pl.ds(pl.multiple_of(at * 256, 256), 256)
-            total = None
-            for low in (0, 1):
-                feats = pl.ds(pl.multiple_of((low * 4 + pair) * PAIR, PAIR), PAIR)
-                a = ctx_all[:, :, feats].reshape(NX * ROWS, PAIR)
-                b = w_all[block, low, pl.ds(pair * 2, 2), :, :, cols].reshape(PAIR, 256)
-                term = jnp.dot(a, b, preferred_element_type=F32)
-                total = term if total is None else total + term
+            a = jnp.concatenate(
+                [
+                    ctx_all[:, :, pl.ds(pl.multiple_of((low * 4 + pair) * PAIR, PAIR), PAIR)].reshape(NX * ROWS, PAIR)
+                    for low in (0, 1)
+                ],
+                axis=1,
+            )
+            b = jnp.concatenate(
+                [w_all[block, low, pl.ds(pair * 2, 2), :, :, cols].reshape(PAIR, 256) for low in (0, 1)], axis=0
+            )
+            total = jnp.dot(a, b, preferred_element_type=F32)
             if start:
                 hid[block, :, cols] = total
             else:
@@ -241,6 +248,9 @@
     a_in(0)
     b_in(1)
     relay(0)
+
+    a_in(1)
+    b_in(2)
 
     arrived(ctx_part(ctx_all.at[left], 0), cr.at[0])
     c_out.append(
@@ -250,16 +260,8 @@
     c_out.append(
         send(ctx_part(ctx_all.at[right], 1), ctx_part(ctx_all.at[right], 1), cs.at[5], cr.at[5], x_dev(3))
     )
-    a_in(1)
-    b_in(2)
     relay(1)
     hand(0)
-
-    for way in (0, 1):
-        for block in (0, 1):
-            arrived(transit.at[way, block], rr.at[way * 2 + block])
-        spot = res_in.at[left if way == 0 else right, :, pl.ds(way * HALF, HALF)]
-        r_out.append(send(transit.at[way], spot, rs.at[8 + way], rr.at[8 + way], x_dev(1 if way == 0 else 3)))
 
     own[3].wait()
     own[4].wait()
@@ -285,32 +287,38 @@
 
     a_in(2)
     b_in(3)
+    for copy in c_out[:4]:
+        copy.wait_send()
+    res_far()
     relay(2)
     hand(1)
-
+    for copy in c_out[4:]:
+        copy.wait_send()
+    res_near()
+    a_in(3)
+    b_in(4)
     own[0].wait()
     arrived(ctx_part(ctx_all.at[left], 1), cr.at[1])
     arrived(ctx_part(ctx_all.at[right], 0), cr.at[2])
     arrived(ctx_part(ctx_all.at[opposite], 0), cr.at[4])
     arrived(ctx_part(ctx_all.at[opposite], 1), cr.at[5])
+    relay(3)
+    hand(2)
 
     base = z // 2
     odd = lax.rem(z, 2)
     handed(0)
     handed(1)
     multiply(base, True)
-    a_in(3)
-    b_in(4)
-    relay(3)
-    hand(2)
-    handed(2)
-    multiply(lax.rem(base + 3 + 2 * odd, 4), False)
+    res_relay()
     a_in(4)
     relay(4)
     hand(3)
+    handed(2)
+    multiply(lax.rem(base + 3 + 2 * odd, 4), False)
+    hand(4)
     handed(3)
     multiply(lax.rem(base + 1 + 2 * odd, 4), False)
-    hand(4)
     handed(4)
     multiply(lax.rem(base + 2, 4), False)
 
@@ -421,7 +429,7 @@
         begin = end
     out[2:3, :VOCAB] = proteins
 
-    for copy in w_out + c_out + r_out + n_out + z_out + b_out + h_out + g_out:
+    for copy in w_out + r_out + n_out + z_out + b_out + h_out + g_out:
         copy.wait_send()
     for k in range(3):
         arrived(part.at[k], ps.at[k])
@@ -429,6 +437,12 @@
     arrived(dp_in, ds_.at[0])
     packed_row = dp_send[dp] + jnp.sum(dp_in[...], axis=0)
     out[1:2, :VOCAB] = packed_row
+
+
+def deal(rows, scores, packed, proteins):
+    scores[...] = rows[0:1, :ROWS].reshape(ROWS)
+    packed[...] = rows[1:2, :HALF].reshape(HALF)
+    proteins[...] = rows[2:3, :4].reshape(4)
 
 
 def shards(context, residual, out_weight, norm_gain, norm_bias, head_weight, targets, packing, lengths):
@@ -477,7 +491,12 @@
         context, residual, out_weight, head_weight,
         norm_gain, norm_bias, targets, packing, lengths,
     )
-    return rows[0, :ROWS], rows[1, :HALF], rows[2, :4]
+    return pl.pallas_call(
+        deal,
+        out_shape=tuple(jax.ShapeDtypeStruct((n,), F32) for n in (ROWS, HALF, 4)),
+        in_specs=[vmem],
+        out_specs=(vmem, vmem, vmem),
+    )(rows)
 
 
 def solution(mesh):

time: 174 us -> 135 us (0.78)
  Pallas kernels: 169 us -> 134 us
  local copies, waits for them, and re-layouts: 3.65 us -> 0 us
    pallas_call x1, Pallas kernels: 169 us -> 133 us  [shards(): pl.pallas_call(kernel, out_shape=jax.ShapeDtypeStruct((8, 256), F32), in_...]
    squeeze x2 -> x0, local copies, waits for them, and re-layouts: 2.39 us -> none  [shards(): return (rows[0, :ROWS], rows[1, :HALF], rows[2, :4])]
where the time goes in v3:
time: 135 us
  Pallas kernels  134 us (99%)
    pallas_call x1, Pallas kernels, shards(): pl.pallas_call(kernel, out_shape=jax.ShapeDtypeStruct((8, 256), F32), in_...  133 us

profile of v3, /device:TPU:1, one launch (start us, length us, event | category | flops | bytes accessed | tf_op | source)
XLA Modules:
  0.0 135.0 jit_solution(17503810580706791946)
XLA Ops:
  0.6 133.1 %shard_map.112.rows = f32[8,256]{1,0:T(8,128)} custom-call(bf16[192,5120]{1,0:T(8,128)(2,1)} %ctx.1, bf16[192,10240]{1,0:T(8,128)(2,1)} %res.1, bf16[160,1280]{1,0:T(8,128)(2,1)} %w.1, bf16[1280,128]{1,0:T(8,128)(2,1)} %head.1, f32[1280]{0:T(1024)} %gain.1, f32[1280]{0:T(1024)} %bias.1, s32[192]{0:T(256)} %targets.1, s32[2,192]{1,0:T(2,128)} %packing.1, s32[4]{0:T(128)} %lens.1), custom_call_target="tpu_custom_call" | custom-call | tf_op jit(solution)/shard_map/pallas_call | solution.py:452
  133.7 1.3 shard_map.113

commit v4 on v3

--- a/solution.py
+++ b/solution.py
@@ -71,6 +71,30 @@
     def piece(of_y, at, rows):
         return w_all.at[of_y // 2, lax.rem(of_y, 2), at, core, rows]
 
+    def ctx_part(ref, part_of):
+        return ref.at[pl.ds(part_of * HALF, HALF)]
+
+    c_out = []
+
+    def send_ctx(way, part_of):
+        at = way * 2 + part_of
+        c_out.append(
+            send(
+                ctx_part(ctx, part_of), ctx_part(ctx_all.at[x], part_of), cs.at[at], cr.at[at],
+                x_dev(1 if way == 0 else 3),
+            )
+        )
+
+    def columns(block, to):
+        return pl.ds(pl.multiple_of((block * NX + to) * NB, NB), NB)
+
+    opposite = lax.rem(x + 2, NX)
+    r_out = []
+    send_ctx(0, 0)
+    send_ctx(1, 1)
+    send_ctx(0, 1)
+    send_ctx(1, 0)
+
     b_out = []
     w_out = [send(w.at[first], piece(y, z, first), ws.at[k - 1], wr.at[k - 1], y_dev(k)) for k in (1, 2, 3)]
     for way, to in ((0, z_dev(1)), (1, z_dev(NZ - 1))):
@@ -80,29 +104,6 @@
     w_own = pltpu.make_async_copy(w, w_all.at[yh, yl, z, core], lsem.at[0])
     w_own.start()
 
-    def ctx_part(ref, part_of):
-        return ref.at[pl.ds(part_of * HALF, HALF)]
-
-    c_out = []
-
-    def send_ctx(way, part_of):
-        at = way * 2 + part_of
-        c_out.append(
-            send(
-                ctx_part(ctx, part_of), ctx_part(ctx_all.at[x], part_of), cs.at[at], cr.at[at],
-                x_dev(1 if way == 0 else 3),
-            )
-        )
-
-    def columns(block, to):
-        return pl.ds(pl.multiple_of((block * NX + to) * NB, NB), NB)
-
-    opposite = lax.rem(x + 2, NX)
-    r_out = []
-    send_ctx(0, 0)
-    send_ctx(1, 1)
-    send_ctx(0, 1)
-    send_ctx(1, 0)
 
     def res_far():
         for way in (0, 1):
@@ -115,13 +116,14 @@
                     )
                 )
 
-    def res_near():
+    def res_near(half):
+        rows = pl.ds(half * HALF, HALF)
         for way in (0, 1):
             for block in (0, 1):
-                at = 4 + way * 2 + block
+                at = 4 + 4 * half + 2 * way + block
                 r_out.append(
                     send(
-                        res.at[:, columns(block, right if way == 0 else left)], res_in.at[x, block],
+                        res.at[rows, columns(block, right if way == 0 else left)], res_in.at[x, block, rows],
                         rs.at[at], rr.at[at], x_dev(1 if way == 0 else 3),
                     )
                 )
@@ -129,9 +131,12 @@
     def res_relay():
         for way in (0, 1):
             for block in (0, 1):
-                arrived(transit.at[way, block], rr.at[way * 2 + block])
-            spot = res_in.at[left if way == 0 else right, :, pl.ds(way * HALF, HALF)]
-            r_out.append(send(transit.at[way], spot, rs.at[8 + way], rr.at[8 + way], x_dev(1 if way == 0 else 3)))
+                at = way * 2 + block
+                arrived(transit.at[way, block], rr.at[at])
+                spot = res_in.at[left if way == 0 else right, block, pl.ds(way * HALF, HALF)]
+                r_out.append(
+                    send(transit.at[way, block], spot, rs.at[12 + at], rr.at[12 + at], x_dev(1 if way == 0 else 3))
+                )
 
     partner = y_dev(2)
     n_out = [
@@ -294,7 +299,7 @@
     hand(1)
     for copy in c_out[4:]:
         copy.wait_send()
-    res_near()
+    res_near(0)
     a_in(3)
     b_in(4)
     own[0].wait()
@@ -316,55 +321,64 @@
     hand(3)
     handed(2)
     multiply(lax.rem(base + 3 + 2 * odd, 4), False)
+    res_near(1)
     hand(4)
     handed(3)
     multiply(lax.rem(base + 1 + 2 * odd, 4), False)
     handed(4)
     multiply(lax.rem(base + 2, 4), False)
 
-    own[1].wait()
-    own[2].wait()
-    for way in (0, 1):
-        frm = left if way == 0 else right
+    def half_block(k, half):
+        rows_of = lax.rem(x + k + 1, NX)
+        at = pl.ds(pl.multiple_of(rows_of * ROWS + half * HALF, HALF), HALF)
+        within = pl.ds(half * HALF, HALF)
+        row_sum = jnp.zeros((HALF, 1), F32)
         for block in (0, 1):
-            arrived(res_in.at[frm, block], rr.at[4 + way * 2 + block])
-    for way in (0, 1):
-        arrived(res_in.at[opposite, :, pl.ds(way * HALF, HALF)], rr.at[8 + way])
-
-    def block_part(k):
-        rows_of = lax.rem(x + k + 1, NX)
-        at = pl.ds(pl.multiple_of(rows_of * ROWS, ROWS), ROWS)
-        row_sum = jnp.zeros((ROWS, 1), F32)
-        for block in (0, 1):
-            full = hid[block, at] + res_in[rows_of, block].astype(F32)
+            full = hid[block, at] + res_in[rows_of, block, within].astype(F32)
             hid[block, at] = full
             row_sum += jnp.sum(full, axis=1, keepdims=True)
         mean = row_sum * (1.0 / LOCAL_WIDTH)
-        square = jnp.zeros((ROWS, 1), F32)
-        product = jnp.zeros((ROWS, VOCAB), F32)
+        square = jnp.zeros((HALF, 1), F32)
+        product = jnp.zeros((2 * HALF, VOCAB), F32)
         for block in (0, 1):
             off = hid[block, at] - mean
             square += jnp.sum(off * off, axis=1, keepdims=True)
             scaled = off * gain_all[block]
             top = scaled.astype(BF16)
             rest = (scaled - top.astype(F32)).astype(BF16)
-            product += jnp.dot(top, head_all[block], preferred_element_type=F32)
-            product += jnp.dot(rest, head_all[block], preferred_element_type=F32)
-        lane = lax.broadcasted_iota(jnp.int32, (ROWS, VOCAB), 1)
+            product += jnp.dot(
+                jnp.concatenate([top, rest], axis=0), head_all[block], preferred_element_type=F32
+            )
+        lane = lax.broadcasted_iota(jnp.int32, (HALF, VOCAB), 1)
         both = jnp.concatenate(
-            [jnp.where(lane == 0, mean, square), jnp.zeros((256 - ROWS, VOCAB), F32)], axis=0
+            [jnp.where(lane == 0, mean, square), jnp.zeros((VOCAB - HALF, VOCAB), F32)], axis=0
         )
-        both = jnp.transpose(both)[:8]
-        part[k, :ROWS] = product
-        part[k, ROWS : ROWS + 8] = both[:, :VOCAB]
-        part[k, ROWS + 8 :] = both[:, VOCAB:]
-
-    @pl.loop(0, 3)
-    def _(k):
-        block_part(k)
-        send(part.at[k], part_in.at[k], ps.at[k], pr.at[k], x_dev(k + 1))
-
-    block_part(3)
+        part[k, half, :HALF] = product[:HALF] + product[HALF:]
+        part[k, half, HALF:] = jnp.transpose(both)[:8]
+        if k < 3:
+            p_out.append(
+                send(part.at[k, half], part_in.at[k, half], ps.at[2 * k + half], pr.at[2 * k + half], x_dev(k + 1))
+            )
+
+    p_out = []
+    own[1].wait()
+    own[2].wait()
+    for half in (0, 1):
+        half_block(3, half)
+    for copy in w_out + n_out + z_out + b_out + h_out + g_out:
+        copy.wait_send()
+    for half in (0, 1):
+        for block in (0, 1):
+            arrived(res_in.at[opposite, block, pl.ds(half * HALF, HALF)], rr.at[12 + 2 * half + block])
+        half_block(1, half)
+    for half in (0, 1):
+        for way in (0, 1):
+            for block in (0, 1):
+                arrived(
+                    res_in.at[left if way == 0 else right, block, pl.ds(half * HALF, HALF)],
+                    rr.at[4 + 4 * half + 2 * way + block],
+                )
+            half_block(2 if way == 0 else 0, half)
 
     info[...] = jnp.full((8, 256), -1, jnp.int32)
     info[0:1, :ROWS] = targets[...].reshape(1, ROWS)
@@ -372,21 +386,23 @@
     label = jnp.transpose(jnp.broadcast_to(info[0:1, :].astype(F32), (VOCAB, 256)))[:ROWS]
     for k in range(3):
         arrived(g_in.at[k], gr.at[k])
-        arrived(part_in.at[k], pr.at[k])
+        for half in (0, 1):
+            arrived(part_in.at[k, half], pr.at[2 * k + half])
     parts = [part[3]] + [part_in[k] for k in range(3)]
     sums = [g_own[...]] + [g_in[k] for k in range(3)]
-    stats = [jnp.concatenate([p[ROWS : ROWS + 8], p[ROWS + 8 :]], axis=1) for p in parts]
+    stats = [jnp.concatenate([p[0, HALF:], p[1, HALF:]], axis=1) for p in parts]
     center = (stats[0][0:1] + stats[1][0:1] + stats[2][0:1] + stats[3][0:1]) * 0.25
     total_square = stats[0][1:2] + stats[1][1:2] + stats[2][1:2] + stats[3][1:2]
     away = [st[0:1] - center for st in stats]
     for a in away:
         total_square += LOCAL_WIDTH * (a * a)
     inverse = lax.rsqrt(total_square * (1.0 / WIDTH) + EPS)
-    by_row = jnp.transpose(jnp.concatenate([inverse, *away, jnp.zeros((VOCAB - 5, 256), F32)], axis=0))[:ROWS]
+    by_row = jnp.transpose(jnp.concatenate([inverse, *away, jnp.zeros((VOCAB - 5, 256), F32)], axis=0))
+    by_row = jnp.concatenate([by_row[:HALF], by_row[VOCAB : VOCAB + HALF]], axis=0)
     logits = jnp.zeros((ROWS, VOCAB), F32)
     shift = jnp.zeros((1, VOCAB), F32)
     for i in range(4):
-        logits += parts[i][:ROWS] + by_row[:, i + 1 : i + 2] * sums[i][0:1]
+        logits += parts[i][:, :HALF].reshape(ROWS, VOCAB) + by_row[:, i + 1 : i + 2] * sums[i][0:1]
         shift += sums[i][4:5]
     logits = logits * by_row[:, 0:1] + shift
     largest = jnp.max(logits, axis=1, keepdims=True)
@@ -407,10 +423,12 @@
         lhs = lhs - top.astype(F32)
     dp_send[...] = packed.reshape(NDP, 1, VOCAB)
 
-    @pl.loop(1, NDP)
-    def _(k):
+    def deliver(k):
         to = lax.rem(dp + k, NDP)
         send(dp_send.at[to], dp_in.at[k - 1], ds_.at[0], dr.at[0], (to, tensor))
+
+    pl.loop(8, NDP)(deliver)
+    pl.loop(1, 8)(deliver)
 
     live_score = jnp.where(group >= 0, score_rows[0:1], 0.0)
     out[0:1] = live_score
@@ -429,10 +447,8 @@
         begin = end
     out[2:3, :VOCAB] = proteins
 
-    for copy in w_out + r_out + n_out + z_out + b_out + h_out + g_out:
+    for copy in r_out + p_out:
         copy.wait_send()
-    for k in range(3):
-        arrived(part.at[k], ps.at[k])
     arrived(dp_in, dr.at[0])
     arrived(dp_in, ds_.at[0])
     packed_row = dp_send[dp] + jnp.sum(dp_in[...], axis=0)
@@ -465,14 +481,14 @@
             pltpu.VMEM((2, 1, NB), F32),
             pltpu.VMEM((8, VOCAB), F32),
             pltpu.VMEM((3, 8, VOCAB), F32),
-            pltpu.VMEM((4, ROWS + 16, VOCAB), F32),
-            pltpu.VMEM((3, ROWS + 16, VOCAB), F32),
+            pltpu.VMEM((4, 2, HALF + 8, VOCAB), F32),
+            pltpu.VMEM((3, 2, HALF + 8, VOCAB), F32),
             pltpu.VMEM((8, 256), jnp.int32),
             pltpu.VMEM((NDP, 1, VOCAB), F32),
             pltpu.VMEM((NDP - 1, 1, VOCAB), F32),
             dma((7,)),
             dma((6,)), dma((6,)),
-            dma((10,)), dma((10,)),
+            dma((16,)), dma((16,)),
             dma((3,)), dma((3,)),
             dma((8,)), dma((8,)),
             dma((8,)), dma((8,)),
@@ -481,7 +497,7 @@
             dma((8,)), dma((8,)),
             dma((3,)), dma((3,)),
             dma((3,)), dma((3,)),
-            dma((3,)), dma((3,)),
+            dma((6,)), dma((6,)),
             dma((1,)), dma((1,)),
         ],
         compiler_params=pltpu.CompilerParams(

time: 135 us -> 134 us (level)
  no operation moved by 1% of the time
where the time goes in v4:
time: 134 us
  Pallas kernels  133 us (99%)
    pallas_call x1, Pallas kernels, shards(): pl.pallas_call(kernel, out_shape=jax.ShapeDtypeStruct((8, 256), F32), in_...  132 us

profile of v4, /device:TPU:1, one launch (start us, length us, event | category | flops | bytes accessed | tf_op | source)
XLA Modules:
  0.0 133.8 jit_solution(18330929713845211267)
XLA Ops:
  0.6 131.9 %shard_map.112.rows = f32[8,256]{1,0:T(8,128)} custom-call(bf16[192,5120]{1,0:T(8,128)(2,1)} %ctx.1, bf16[192,10240]{1,0:T(8,128)(2,1)} %res.1, bf16[160,1280]{1,0:T(8,128)(2,1)} %w.1, bf16[1280,128]{1,0:T(8,128)(2,1)} %head.1, f32[1280]{0:T(1024)} %gain.1, f32[1280]{0:T(1024)} %bias.1, s32[192]{0:T(256)} %targets.1, s32[2,192]{1,0:T(2,128)} %packing.1, s32[4]{0:T(128)} %lens.1), custom_call_target="tpu_custom_call" | custom-call | tf_op jit(solution)/shard_map/pallas_call | solution.py:468
  132.6 1.3 shard_map.113

commit v5 on v4

--- a/solution.py
+++ b/solution.py
@@ -21,10 +21,10 @@
 
 
 def kernel(
-    ctx, res, w, head, gain, bias, targets, packing, lens,
+    ctx, res, w, head, gain, bias, targets_in, packing_in, lens_in,
     out,
     ctx_all, res_in, transit, w_all, hid, head_all, gain_all, bias_all,
-    g_own, g_in, part, part_in, info, dp_send, dp_in,
+    g_own, g_in, part, part_in, info, targets, packing, lens, dp_send, dp_in,
     lsem, cs, cr, rs, rr, ws, wr, zs, zr, bs, br, us, ur, os, or_, hs, hr, ns, nr, gs, gr, ps, pr, ds_, dr,
 ):
     dp = lax.axis_index("dp")
@@ -151,6 +151,9 @@
         pltpu.make_async_copy(head, head_all.at[yh], lsem.at[4]),
         pltpu.make_async_copy(gain, gain_all.at[yh, 0], lsem.at[5]),
         pltpu.make_async_copy(bias, bias_all.at[yh, 0], lsem.at[6]),
+        pltpu.make_async_copy(targets_in, targets, lsem.at[7]),
+        pltpu.make_async_copy(packing_in, packing, lsem.at[8]),
+        pltpu.make_async_copy(lens_in, lens, lsem.at[9]),
     ]
     for copy in own:
         copy.start()
@@ -361,8 +364,8 @@
             )
 
     p_out = []
-    own[1].wait()
-    own[2].wait()
+    for copy in own[1:3] + own[6:]:
+        copy.wait()
     for half in (0, 1):
         half_block(3, half)
     for copy in w_out + n_out + z_out + b_out + h_out + g_out:
@@ -384,6 +387,10 @@
     info[0:1, :ROWS] = targets[...].reshape(1, ROWS)
     info[1:3, :ROWS] = packing[...]
     label = jnp.transpose(jnp.broadcast_to(info[0:1, :].astype(F32), (VOCAB, 256)))[:ROWS]
+    group = info[1:2, :]
+    place = info[2:3, :]
+    chosen = jnp.where(lax.broadcasted_iota(jnp.int32, (VOCAB, 256), 0) == place, 1.0, 0.0).astype(BF16)
+    to_group = lax.broadcasted_iota(jnp.int32, (NDP, 256), 0) == group
     for k in range(3):
         arrived(g_in.at[k], gr.at[k])
         for half in (0, 1):
@@ -412,10 +419,7 @@
     score = jnp.broadcast_to(picked - log_total, (ROWS, VOCAB))
     score_rows = jnp.transpose(jnp.concatenate([score, jnp.zeros((256 - ROWS, VOCAB), F32)], axis=0))
 
-    group = info[1:2, :]
-    place = info[2:3, :]
-    lhs = jnp.where(lax.broadcasted_iota(jnp.int32, (NDP, 256), 0) == group, score_rows[:NDP], 0.0)
-    chosen = jnp.where(lax.broadcasted_iota(jnp.int32, (VOCAB, 256), 0) == place, 1.0, 0.0).astype(BF16)
+    lhs = jnp.where(to_group, score_rows[:NDP], 0.0)
     packed = jnp.zeros((NDP, VOCAB), F32)
     for _ in range(3):
         top = lhs.astype(BF16)
@@ -468,7 +472,7 @@
     rows = pl.pallas_call(
         kernel,
         out_shape=jax.ShapeDtypeStruct((8, 256), F32),
-        in_specs=[any_] * 6 + [vmem, vmem, pl.BlockSpec(memory_space=pltpu.SMEM)],
+        in_specs=[any_] * 9,
         out_specs=vmem,
         scratch_shapes=[
             pltpu.VMEM((NX, ROWS, CTX), BF16),
@@ -484,9 +488,12 @@
             pltpu.VMEM((4, 2, HALF + 8, VOCAB), F32),
             pltpu.VMEM((3, 2, HALF + 8, VOCAB), F32),
             pltpu.VMEM((8, 256), jnp.int32),
+            pltpu.VMEM((ROWS,), jnp.int32),
+            pltpu.VMEM((2, ROWS), jnp.int32),
+            pltpu.SMEM((4,), jnp.int32),
             pltpu.VMEM((NDP, 1, VOCAB), F32),
             pltpu.VMEM((NDP - 1, 1, VOCAB), F32),
-            dma((7,)),
+            dma((10,)),
             dma((6,)), dma((6,)),
             dma((16,)), dma((16,)),
             dma((3,)), dma((3,)),

time: 134 us -> 133 us (level)
  no operation moved by 1% of the time
where the time goes in v5:
time: 133 us
  Pallas kernels  132 us (99%)
    pallas_call x1, Pallas kernels, shards(): pl.pallas_call(kernel, out_shape=jax.ShapeDtypeStruct((8, 256), F32), in_...  131 us

profile of v5, /device:TPU:1, one launch (start us, length us, event | category | flops | bytes accessed | tf_op | source)
XLA Modules:
  0.0 133.1 jit_solution(7204275711837400783)
XLA Ops:
  0.6 131.2 %shard_map.112.rows = f32[8,256]{1,0:T(8,128)} custom-call(bf16[192,5120]{1,0:T(8,128)(2,1)} %ctx.1, bf16[192,10240]{1,0:T(8,128)(2,1)} %res.1, bf16[160,1280]{1,0:T(8,128)(2,1)} %w.1, bf16[1280,128]{1,0:T(8,128)(2,1)} %head.1, f32[1280]{0:T(1024)} %gain.1, f32[1280]{0:T(1024)} %bias.1, s32[192]{0:T(256)} %targets_in.1, s32[2,192]{1,0:T(2,128)} %packing_in.1, ...), custom_call_target="tpu_custom_call" | custom-call | tf_op jit(solution)/shard_map/pallas_call | solution.py:472
  131.8 1.3 shard_map.113

commit v6 on v5

--- a/solution.py
+++ b/solution.py
@@ -393,31 +393,34 @@
     to_group = lax.broadcasted_iota(jnp.int32, (NDP, 256), 0) == group
     for k in range(3):
         arrived(g_in.at[k], gr.at[k])
-        for half in (0, 1):
+    sums = [g_own[...]] + [g_in[k] for k in range(3)]
+    shift = sums[0][4:5] + sums[1][4:5] + sums[2][4:5] + sums[3][4:5]
+    token = lax.broadcasted_iota(jnp.int32, (HALF, VOCAB), 1).astype(F32)
+
+    def score_of(half):
+        for k in range(3):
             arrived(part_in.at[k, half], pr.at[2 * k + half])
-    parts = [part[3]] + [part_in[k] for k in range(3)]
-    sums = [g_own[...]] + [g_in[k] for k in range(3)]
-    stats = [jnp.concatenate([p[0, HALF:], p[1, HALF:]], axis=1) for p in parts]
-    center = (stats[0][0:1] + stats[1][0:1] + stats[2][0:1] + stats[3][0:1]) * 0.25
-    total_square = stats[0][1:2] + stats[1][1:2] + stats[2][1:2] + stats[3][1:2]
-    away = [st[0:1] - center for st in stats]
-    for a in away:
-        total_square += LOCAL_WIDTH * (a * a)
-    inverse = lax.rsqrt(total_square * (1.0 / WIDTH) + EPS)
-    by_row = jnp.transpose(jnp.concatenate([inverse, *away, jnp.zeros((VOCAB - 5, 256), F32)], axis=0))
-    by_row = jnp.concatenate([by_row[:HALF], by_row[VOCAB : VOCAB + HALF]], axis=0)
-    logits = jnp.zeros((ROWS, VOCAB), F32)
-    shift = jnp.zeros((1, VOCAB), F32)
-    for i in range(4):
-        logits += parts[i][:, :HALF].reshape(ROWS, VOCAB) + by_row[:, i + 1 : i + 2] * sums[i][0:1]
-        shift += sums[i][4:5]
-    logits = logits * by_row[:, 0:1] + shift
-    largest = jnp.max(logits, axis=1, keepdims=True)
-    log_total = largest + jnp.log(jnp.sum(jnp.exp(logits - largest), axis=1, keepdims=True))
-    token = lax.broadcasted_iota(jnp.int32, (ROWS, VOCAB), 1).astype(F32)
-    picked = jnp.sum(jnp.where(token == label, logits, 0.0), axis=1, keepdims=True)
-    score = jnp.broadcast_to(picked - log_total, (ROWS, VOCAB))
-    score_rows = jnp.transpose(jnp.concatenate([score, jnp.zeros((256 - ROWS, VOCAB), F32)], axis=0))
+        parts = [part[3, half]] + [part_in[k, half] for k in range(3)]
+        stats = [p[HALF:] for p in parts]
+        center = (stats[0][0:1] + stats[1][0:1] + stats[2][0:1] + stats[3][0:1]) * 0.25
+        total_square = stats[0][1:2] + stats[1][1:2] + stats[2][1:2] + stats[3][1:2]
+        away = [st[0:1] - center for st in stats]
+        for a in away:
+            total_square += LOCAL_WIDTH * (a * a)
+        inverse = lax.rsqrt(total_square * (1.0 / WIDTH) + EPS)
+        by_row = jnp.transpose(jnp.concatenate([inverse, *away, jnp.zeros((VOCAB - 5, VOCAB), F32)], axis=0))[:HALF]
+        logits = jnp.zeros((HALF, VOCAB), F32)
+        for i in range(4):
+            logits += parts[i][:HALF] + by_row[:, i + 1 : i + 2] * sums[i][0:1]
+        logits = logits * by_row[:, 0:1] + shift
+        largest = jnp.max(logits, axis=1, keepdims=True)
+        log_total = largest + jnp.log(jnp.sum(jnp.exp(logits - largest), axis=1, keepdims=True))
+        wanted = label[half * HALF : (half + 1) * HALF]
+        picked = jnp.sum(jnp.where(token == wanted, logits, 0.0), axis=1, keepdims=True)
+        return jnp.broadcast_to(picked - log_total, (HALF, VOCAB))
+
+    score = [score_of(0), score_of(1)]
+    score_rows = jnp.transpose(jnp.concatenate(score + [jnp.zeros((256 - ROWS, VOCAB), F32)], axis=0))
 
     lhs = jnp.where(to_group, score_rows[:NDP], 0.0)
     packed = jnp.zeros((NDP, VOCAB), F32)

time: 133 us -> 133 us (level)
  no operation moved by 1% of the time
where the time goes in v6:
time: 133 us
  Pallas kernels  132 us (99%)
    pallas_call x1, Pallas kernels, shards(): pl.pallas_call(kernel, out_shape=jax.ShapeDtypeStruct((8, 256), F32), in_...  131 us

profile of v6, /device:TPU:1, one launch (start us, length us, event | category | flops | bytes accessed | tf_op | source)
XLA Modules:
  0.0 133.0 jit_solution(2159308574871344021)
XLA Ops:
  0.6 131.0 %shard_map.112.rows = f32[8,256]{1,0:T(8,128)} custom-call(bf16[192,5120]{1,0:T(8,128)(2,1)} %ctx.1, bf16[192,10240]{1,0:T(8,128)(2,1)} %res.1, bf16[160,1280]{1,0:T(8,128)(2,1)} %w.1, bf16[1280,128]{1,0:T(8,128)(2,1)} %head.1, f32[1280]{0:T(1024)} %gain.1, f32[1280]{0:T(1024)} %bias.1, s32[192]{0:T(256)} %targets_in.1, s32[2,192]{1,0:T(2,128)} %packing_in.1, ...), custom_call_target="tpu_custom_call" | custom-call | tf_op jit(solution)/shard_map/pallas_call | solution.py:475
  131.7 1.3 shard_map.113
